TPU v7x, 32 devices: a whole 2x2x4 slice. The times are simulated.
32 devices in a mesh: row: 4 (over x, core), col: 8 (over z, y).
Axes of the slice: x: 2, y: 2, z: 4, core: 2. Of those that a mesh axis runs over, the one named last changes fastest.
Arguments:
- observations: float32 [1024, 8192], P('row', 'col'), may hold values from -6 to 6
- omega: float32 [8, 3, 16, 128, 128], P('col'), as said below
- block_slots: int32 [8, 3, 16], P('col'), may hold values from -1 to 63, as said below
Outputs:
- new_omega: float32 [8, 3, 16, 128, 128], P('col', None, 'row')
Inputs may be any that keep to these rules, and one draw needn't show every extreme that they name: `block_slots`: active slots come first in each tile. The pattern is symmetric: slot j of [t, 2] and slot j of [t + 1, 0] (modulo 8) name mirrored blocks, a and b swapped; in [t, 1] the 8 diagonal blocks come first in order, then mirrored pairs side by side. Some tile has all 16 slots active. `omega`: the blocks of active slots form one symmetric matrix: the block of slot j of [t, 2] is the transpose of that of slot j of [t + 1, 0], mirrored pairs of [t, 1] are transposes of each other, and diagonal blocks are symmetric with diagonal entries of 0.8 or more. Empty slots hold arbitrary values.
All inputs are finite; a program needn't handle non-finite values.
Results may differ from a plain program's by a relative error of at most 0.0003.
Values sent between devices are 32-bit elements; how exact they have to be, the bound alone decides.
A program may use at most 128 MiB of HBM per device.

v0:
```python
import jax
import jax.numpy as jnp
from jax import lax
from jax.sharding import PartitionSpec as P

TILE = 1024
BLK = 128


step_size = 0.5
penalty = 0.1
highest = lax.Precision.HIGHEST


def shifted(value, axis, steps):
    count = lax.axis_size(axis)
    pairs = [(source, (source + steps) % count) for source in range(count)]
    return lax.ppermute(value, axis, pairs)


def local_terms(nearby, omega_strip, slot_ids):
    tile_blocks = TILE // BLK
    active = slot_ids >= 0
    row_pick = jax.nn.one_hot(
        jnp.where(active, slot_ids // tile_blocks, -1), tile_blocks, dtype=jnp.float32
    )
    col_pick = jax.nn.one_hot(
        jnp.where(active, slot_ids % tile_blocks, -1), tile_blocks, dtype=jnp.float32
    )
    chosen = jnp.einsum("ejn,epnk->ejpk", row_pick, nearby, precision=highest)
    product = jnp.einsum("ejpk,ejkl->ejpl", chosen, omega_strip, precision=highest)
    residual = jnp.einsum("ejn,ejpl->pnl", col_pick, product, precision=highest)
    picked = jnp.einsum("ejn,pnl->ejpl", col_pick, residual, precision=highest)
    return jnp.einsum("ejpk,ejpl->ejkl", chosen, picked, precision=highest)


def mirror_inner(forward_centre, centre_ids):
    tile_blocks = TILE // BLK
    active = centre_ids >= 0
    flipped = jnp.where(
        active, centre_ids % tile_blocks * tile_blocks + centre_ids // tile_blocks, -2
    )
    match_table = (
        (centre_ids[..., None, :] == flipped[..., :, None]) & active[..., None, :]
    ).astype(jnp.float32)
    return jnp.einsum("...jk,...kab->...jba", match_table, forward_centre, precision=highest)


def proximal(omega_part, slot_part, smooth):
    tile_blocks = TILE // BLK
    active = slot_part >= 0
    centre_mask = (jnp.arange(3) == 1)[:, None]
    diagonal_block = active & centre_mask & (slot_part // tile_blocks == slot_part % tile_blocks)
    identity = jnp.eye(BLK, dtype=jnp.float32)
    own_diag = jnp.diagonal(omega_part, axis1=-2, axis2=-1)
    safe_diag = jnp.where(diagonal_block[..., None], own_diag, 1.0)
    inverse = jnp.where(diagonal_block[..., None], 1.0 / safe_diag, 0.0)
    gradient = smooth - inverse[..., None] * identity
    trial_step = omega_part - step_size * gradient
    shrunk = jnp.sign(trial_step) * jnp.maximum(jnp.abs(trial_step) - step_size * penalty, 0.0)
    keep_mask = diagonal_block[..., None, None] & (identity > 0.5)
    result = jnp.where(keep_mask, trial_step, shrunk)
    return jnp.where(active[..., None, None], result, 0.0)


def on_device(observations, omega, block_slots):
    tile_blocks = TILE // BLK
    omega_strip = omega[0]
    slot_ids = block_slots[0]
    from_below = shifted(observations, "col", 1)
    from_above = shifted(observations, "col", -1)
    nearby = jnp.stack([from_below, observations, from_above])
    nearby = nearby.reshape(3, observations.shape[0], tile_blocks, BLK)
    forward = local_terms(nearby, omega_strip, slot_ids)
    inner_half = 0.5 * (forward[1] + mirror_inner(forward[1], slot_ids[1]))
    left_part = shifted(forward[2], "col", 1)
    right_part = shifted(forward[0], "col", -1)
    halves = jnp.stack(
        [
            0.5 * (forward[0] + jnp.swapaxes(left_part, 1, 2)),
            inner_half,
            0.5 * (forward[2] + jnp.swapaxes(right_part, 1, 2)),
        ]
    )
    summed = lax.psum_scatter(halves, "row", scatter_dimension=1, tiled=True)
    sample_count = observations.shape[0] * lax.axis_size("row")
    smooth = summed / sample_count
    share_slots = summed.shape[1]
    first_slot = lax.axis_index("row") * share_slots
    omega_share = lax.dynamic_slice_in_dim(omega_strip, first_slot, share_slots, 1)
    slot_share = lax.dynamic_slice_in_dim(slot_ids, first_slot, share_slots, 1)
    return proximal(omega_share, slot_share, smooth)[None]


def solution(mesh):
    return jax.shard_map(
        on_device,
        mesh=mesh,
        in_specs=(P("row", "col"), P("col", None, None, None, None), P("col", None, None)),
        out_specs=P("col", None, "row", None, None),
        check_vma=False,
    )
```

profile of v0, /device:TPU:0, one launch (start us, length us, event | category | flops | bytes accessed | tf_op | source)
XLA Modules:
  0.0 235.9 jit_solution(14006928463318000888)
XLA Ops:
  6.5 0.0 all-reduce.3.cloned.1.call-start
  6.5 3.0 %collective-permute-start = (f32[256,1024]{1,0:T(8,128)}, f32[256,1024]{1,0:T(8,128)S(1)}, u32[]{:S(2)}, u32[]{:S(2)}) collective-permute-start(f32[256,1024]{1,0:T(8,128)} %param.3), channel_id=1, source_target_pairs={{0,1},{1,2},{2,3},{3,4},{4,5},{5,6},{6,7},{7,0},{8,9},{9,10},{10,1... | collective-permute-start | bytes 3145736 | tf_op jit(solution)/shard_map/ppermute | solution.py:18
  9.5 3.0 %collective-permute-start.1 = (f32[256,1024]{1,0:T(8,128)}, f32[256,1024]{1,0:T(8,128)S(1)}, u32[]{:S(2)}, u32[]{:S(2)}) collective-permute-start(f32[256,1024]{1,0:T(8,128)} %param.3), channel_id=1, source_target_pairs={{0,7},{1,0},{2,1},{3,2},{4,3},{5,4},{6,5},{7,6},{8,15},{9,8},{10,9... | collective-permute-start | bytes 3145736 | tf_op jit(solution)/shard_map/ppermute | solution.py:18
  12.5 1.5 copy.50
  14.0 0.7 fusion.43
  14.7 40.0 %collective-permute-done = f32[256,1024]{1,0:T(8,128)S(1)} collective-permute-done((f32[256,1024]{1,0:T(8,128)}, f32[256,1024]{1,0:T(8,128)S(1)}, u32[]{:S(2)}, u32[]{:S(2)}) %collective-permute-start) | collective-permute-done | bytes 1048608 | tf_op jit(solution)/shard_map/ppermute | solution.py:18
  54.7 0.2 copy.49
  54.9 1.9 collective-permute-done.1
  56.8 0.2 copy.51
  57.0 4.6 %fusion.4 = f32[3,16,256,128]{3,1,2,0:T(8,128)} fusion(f32[1,256,8,128]{3,2,1,0:T(8,128)S(1)} %bitcast.141, f32[1,256,8,128]{3,2,1,0:T(8,128)S(1)} %bitcast.139, f32[1,256,8,128]{3,2,1,0:T(8,128)S(1)} %bitcast.140, s32[3,16]{1,0:T(4,128)S(1)} %get-tuple-element.13), kind=kOutput, calls=%fused_computation.5 | convolution fusion | flops 152568192 | bytes 9437376 | tf_op jit(solution)/shard_map/ejn,epnk->ejpk/dot_general | solution.py:30
  61.6 0.0 copy-start.1
  61.6 6.8 %copy.33 = f32[3,16,256,128]{2,3,1,0:T(8,128)} copy(f32[3,16,256,128]{3,1,2,0:T(8,128)} %fusion.4) | data formatting | bytes 12582912 | tf_op jit(solution)/shard_map/ejn,epnk->ejpk/dot_general | solution.py:30
  68.4 0.0 copy-done.1
  68.4 13.2 %fusion.10 = f32[3,16,256,128]{3,2,1,0:T(8,128)S(1)} fusion(f32[3,16,256,128]{2,3,1,0:T(8,128)} %copy.33, f32[1,3,16,128,128]{4,3,2,1,0:T(8,128)S(1)} %copy-done.1), kind=kOutput, calls=%fused_computation.12 | convolution fusion | flops 2415919104 | bytes 15728640 | tf_op jit(solution)/shard_map/ejpk,ejkl->ejpl/dot_general | solution.py:31
  81.6 5.7 %fusion.12 = f32[256,8,128,1]{2,1,0,3:T(8,128)S(1)} fusion(f32[3,16,256,128]{3,2,1,0:T(8,128)S(1)} %fusion.10, s32[3,16]{1,0:T(4,128)S(1)} %get-tuple-element.12), kind=kOutput, calls=%fused_computation.14 | convolution fusion | flops 150995328 | bytes 7340224 | tf_op jit(solution)/shard_map/ejn,ejpl->pnl/dot_general | solution.py:32
  87.3 0.0 copy-start
  87.3 2.7 %fusion.30 = f32[3,16,256,128]{3,1,2,0:T(8,128)S(1)} fusion(f32[256,8,128,1]{2,1,0,3:T(8,128)S(1)} %fusion.12, s32[3,16]{1,0:T(4,128)S(1)} %get-tuple-element.12), kind=kOutput, calls=%fused_computation.42 | convolution fusion | flops 150995328 | bytes 7340224 | tf_op jit(solution)/shard_map/ejn,pnl->ejpl/dot_general | solution.py:33
  90.0 0.1 copy-done
  90.1 7.9 %fusion = f32[3,16,128,128]{3,2,1,0:T(8,128)S(1)} fusion(f32[3,16,256,128]{2,3,1,0:T(8,128)S(1)} %copy-done, f32[3,16,256,128]{3,1,2,0:T(8,128)S(1)} %fusion.30), kind=kOutput, calls=%fused_computation.1 | convolution fusion | flops 2415919104 | bytes 15728640 | tf_op jit(solution)/shard_map/ejpk,ejpl->ejkl/dot_general | solution.py:34
  98.0 0.0 copy-start.3
  98.0 1.8 slice_bitcast_fusion
  99.8 3.5 %collective-permute-start.3 = (f32[16,128,128]{2,1,0:T(8,128)}, f32[16,128,128]{2,1,0:T(8,128)}, u32[]{:S(2)}, u32[]{:S(2)}) collective-permute-start(f32[16,128,128]{2,1,0:T(8,128)} %get-tuple-element.9), channel_id=1, source_target_pairs={{0,7},{1,0},{2,1},{3,2},{4,3},{5,4},{6,5},{7,6},{8,15},{9,8},{10,9... | collective-permute-start | bytes 3145736 | tf_op jit(solution)/shard_map/ppermute | solution.py:18
  103.3 0.0 copy-done.3
  103.4 2.5 %copy.48 = f32[1,16,128,128]{2,3,1,0:T(8,128)} copy(f32[1,16,128,128]{3,2,1,0:T(8,128)} %get-tuple-element.8) | data formatting | bytes 2097152
  105.9 0.0 collective-permute-start.2
  105.9 3.4 %fusion.19 = f32[128,128,16]{1,2,0:T(8,128)} fusion(f32[16,128,128]{2,1,0:T(8,128)} %get-tuple-element.7, s32[16]{0:T(128)S(1)} %slice_bitcast_fusion.2, s32[16]{0:T(128)S(1)} %fusion.51, pred[16]{0:T(512)(128)(4,1)S(1)} %broadcast_compare_fusion.2), kind=kOutput, calls=%fused_computation.24 | convolution fusion | flops 50332160 | bytes 2097296 | tf_op jit(solution)/shard_map/...jk,...kab->...jba/dot_general | solution.py:46
  109.4 2.6 %copy.37 = f32[128,128,16]{0,1,2:T(8,128)} copy(f32[128,128,16]{1,2,0:T(8,128)} %fusion.19) | data formatting | bytes 2097152 | tf_op jit(solution)/shard_map/...jk,...kab->...jba/dot_general | solution.py:46
  111.9 34.4 %collective-permute-done.3 = f32[16,128,128]{2,1,0:T(8,128)} collective-permute-done((f32[16,128,128]{2,1,0:T(8,128)}, f32[16,128,128]{2,1,0:T(8,128)}, u32[]{:S(2)}, u32[]{:S(2)}) %collective-permute-start.3) | collective-permute-done | bytes 1048608 | tf_op jit(solution)/shard_map/ppermute | solution.py:18
  146.3 2.6 %bitcast_add_fusion = f32[16,128,128]{1,2,0:T(8,128)} fusion(f32[16,128,128]{2,1,0:T(8,128)} %collective-permute-done.3, f32[1,16,128,128]{2,3,1,0:T(8,128)} %copy.48), kind=kLoop, calls=%fused_computation.17 | loop fusion | flops 262144 | bytes 3145728 | tf_op jit(solution)/shard_map/add | solution.py:82
  149.0 2.5 %copy.38 = f32[16,128,128]{2,1,0:T(8,128)} copy(f32[16,128,128]{1,2,0:T(8,128)} %bitcast_add_fusion) | data formatting | bytes 2097152 | tf_op jit(solution)/shard_map/add | solution.py:82
  151.5 1.3 multiply_bitcast_fusion
  152.8 0.0 collective-permute-done.2
  152.8 1.8 fusion.18
  154.7 1.8 pad_maximum_fusion
  156.5 0.0 copy-start.2
  156.5 0.0 all-reduce.3.cloned.1.call-update
  156.5 1.9 copy-done.2
  158.4 0.9 dynamic-slice_bitcast_fusion
  159.3 17.5 %copy.39 = f32[3,4,128,128]{1,0,3,2:T(4,128)} copy(f32[3,4,128,128]{3,2,1,0:T(8,128)} %dynamic-slice_bitcast_fusion) | data formatting | bytes 1572864 | tf_op jit(solution)/shard_map/dynamic_slice | solution.py:90
  176.8 2.6 %gather_fusion = f32[128,3,4]{2,1,0:T(4,128)} fusion(f32[3,4,128,128]{1,0,3,2:T(4,128)} %copy.39, s32[128]{0:T(128)S(1)} %or_bitcast_fusion), kind=kCustom, calls=%fused_computation | custom fusion | bytes 13312 | tf_op jit(solution)/shard_map/jit(diagonal)/gather | solution.py:55
  179.4 0.1 constant_dynamic-slice_fusion
  179.5 0.1 bitcast_compare_fusion.3
  179.6 1.0 select_bitcast_fusion.1
  180.6 0.1 copy.40
  180.7 0.0 copy-done.4
  180.7 0.6 dynamic-slice.2
  182.0 44.5 %all-reduce.3.cloned.1.call-done = f32[3,16,128,128]{3,2,1,0:T(8,128)} async-done(((f32[3,16,128,128]{3,2,1,0:T(8,128)}), f32[3,16,128,128]{3,2,1,0:T(8,128)}) %all-reduce.3.cloned.1.call-update) | async-done | bytes 3145744
  226.4 2.6 %select_bitcast_fusion = f32[1,3,4,128,128]{4,3,2,1,0:T(8,128)} fusion(f32[3,16,128,128]{3,2,1,0:T(8,128)} %all-reduce.3.cloned.1.call-done, u32[]{:T(128)S(6)} %multiply.2, f32[128,128]{1,0:T(8,128)S(1)} %get-tuple-element.14, f32[3,4,128]{2,1,0:T(4,128)S(1)} %copy.40, pred[128,128]{1,0:T(8,128)(4,1)S(1)} %get-tuple-element.15, ...), kind=kLoop, calls=%fused_computation.31 | loop fusion | flops 2555904 | bytes 2447392 | tf_op jit(solution)/shard_map/broadcast_in_dim | solution.py:92
  (7 shorter events, 0.1 us)
Async XLA Ops:
  6.5 219.9 %all-reduce.3.cloned.1.call-start = ((), (), s32[]{:S(2)}) async-start(), calls=%async_computation | async-start | bytes 6291456
  6.5 48.2 %collective-permute-start = (f32[256,1024]{1,0:T(8,128)}, f32[256,1024]{1,0:T(8,128)S(1)}, u32[]{:S(2)}, u32[]{:S(2)}) collective-permute-start(f32[256,1024]{1,0:T(8,128)} %param.3), channel_id=1, source_target_pairs={{0,1},{1,2},{2,3},{3,4},{4,5},{5,6},{6,7},{7,0},{8,9},{9,10},{10,1... | collective-permute-start | bytes 3145736 | tf_op jit(solution)/shard_map/ppermute | solution.py:18
  9.5 47.3 %collective-permute-start.1 = (f32[256,1024]{1,0:T(8,128)}, f32[256,1024]{1,0:T(8,128)S(1)}, u32[]{:S(2)}, u32[]{:S(2)}) collective-permute-start(f32[256,1024]{1,0:T(8,128)} %param.3), channel_id=1, source_target_pairs={{0,7},{1,0},{2,1},{3,2},{4,3},{5,4},{6,5},{7,6},{8,15},{9,8},{10,9... | collective-permute-start | bytes 3145736 | tf_op jit(solution)/shard_map/ppermute | solution.py:18
  61.6 6.8 %copy-start.1 = (f32[1,3,16,128,128]{4,3,2,1,0:T(8,128)S(1)}, f32[1,3,16,128,128]{4,3,2,1,0:T(8,128)}, u32[]{:S(2)}) copy-start(f32[1,3,16,128,128]{4,3,2,1,0:T(8,128)} %param.4) | copy-start | bytes 9437188
  87.3 2.8 %copy-start = (f32[3,16,256,128]{2,3,1,0:T(8,128)S(1)}, f32[3,16,256,128]{2,3,1,0:T(8,128)}, u32[]{:S(2)}) copy-start(f32[3,16,256,128]{2,3,1,0:T(8,128)} %copy.33) | copy-start | bytes 18874372
  98.0 5.3 %copy-start.3 = (s32[1,3,16]{2,0,1:T(1,128)S(1)}, s32[1,3,16]{2,0,1:T(1,128)}, u32[]{:S(2)}) copy-start(s32[1,3,16]{2,0,1:T(1,128)} %param.5) | copy-start | bytes 580
  99.8 46.5 %collective-permute-start.3 = (f32[16,128,128]{2,1,0:T(8,128)}, f32[16,128,128]{2,1,0:T(8,128)}, u32[]{:S(2)}, u32[]{:S(2)}) collective-permute-start(f32[16,128,128]{2,1,0:T(8,128)} %get-tuple-element.9), channel_id=1, source_target_pairs={{0,7},{1,0},{2,1},{3,2},{4,3},{5,4},{6,5},{7,6},{8,15},{9,8},{10,9... | collective-permute-start | bytes 3145736 | tf_op jit(solution)/shard_map/ppermute | solution.py:18
  105.9 46.9 %collective-permute-start.2 = (f32[16,128,128]{1,2,0:T(8,128)}, f32[16,128,128]{1,2,0:T(8,128)}, u32[]{:S(2)}, u32[]{:S(2)}) collective-permute-start(f32[16,128,128]{1,2,0:T(8,128)} %bitcast.138), channel_id=1, source_target_pairs={{0,1},{1,2},{2,3},{3,4},{4,5},{5,6},{6,7},{7,0},{8,9},{9,10},{10,1... | collective-permute-start | bytes 3145736 | tf_op jit(solution)/shard_map/ppermute | solution.py:18
  156.5 1.9 copy-start.2
  159.3 21.4 %copy-start.4 = (u32[32]{0:T(128)S(1)}, u32[32]{0:T(128)}, u32[]{:S(2)}) copy-start(u32[32]{0:T(128)} %constant.122) | copy-start | bytes 388
Sparse Core Ops, SparseCore 0:
  156.6 69.7 all-reduce.2
where the time goes:
time: 237 us; the launch traced here: 236 us
  waiting for transfers between devices  121 us (51%)
  local copies, waits for them, and re-layouts  41.9 us (18%)
  matrix products  37.5 us (16%)
  between operations  14.1 us (6%)
  other arithmetic  12.1 us (5%)
  starting transfers between devices  9.54 us (4%)
    ppermute x4, waiting for transfers between devices, shifted(): return lax.ppermute(value, axis, pairs)  76.3 us
    unnamed x2, waiting for transfers between devices  44.5 us
    dynamic_slice x2, local copies, waits for them, and re-layouts, on_device(): lax.dynamic_slice_in_dim(omega_strip, first_slot, share_slots, 1)  18.4 us
    dot_general x1, matrix products, local_terms(): jnp.einsum('ejpk,ejkl->ejpl', chosen, omega_strip, precision=highest)  13.2 us
    ppermute x4, starting transfers between devices, shifted(): return lax.ppermute(value, axis, pairs)  9.54 us
    dot_general x1, matrix products, local_terms(): return jnp.einsum('ejpk,ejpl->ejkl', chosen, picked, precision=highest)  7.91 us
    unnamed x15, local copies, waits for them, and re-layouts  6.96 us
    dot_general x1, local copies, waits for them, and re-layouts, local_terms(): chosen = jnp.einsum('ejn,epnk->ejpk', row_pick, nearby, precision=highest)  6.84 us
  transfers between devices with their start and end apart: 5, of which 4 were waited for; matrix products, arithmetic and copies ran while one was open for 17% of the time, Pallas kernels for 0%

commit v1 on v0

v1 whole, which is shorter than its diff:
```python
import functools

import jax
import jax.numpy as jnp
from jax import lax
from jax.experimental import pallas as pl
from jax.experimental.pallas import tpu as pltpu
from jax.sharding import PartitionSpec as P

MESH = pl.DeviceIdType.MESH
BLK = 128
TB = 8
HALF = 128
CHUNKS = 8

step_size = 0.5
penalty = 0.1
f32, bf16 = jnp.float32, jnp.bfloat16


def split(value):
    high = value.astype(bf16)
    return high, (value - high.astype(f32)).astype(bf16)


def flip(index, mask):
    out, bit = index, 1
    while bit <= mask:
        if mask & bit:
            out = out + bit * (1 - 2 * lax.rem(lax.div(index, bit), 2))
        bit *= 2
    return out


def kernel(
    nr, nc, kmax, tab, obs, omega, out, near, far, xs, xt, wcat, cum, rs, fbuf, rbuf, mrecv,
    near_send, near_recv, far_send, far_recv, row_send, row_recv, mir_send, mir_recv,
):
    samples = obs.shape[0]
    share = kmax // nr
    bits = nr.bit_length() - 1
    r, c = lax.axis_index("row"), lax.axis_index("col")
    odd = lax.rem(c, 2)
    near_col = c + 1 - 2 * odd
    far_col = lax.rem(c - 1 + 2 * odd + nc, nc)
    relay_to = lax.rem(c + 2 - 4 * odd + nc, nc)
    relay_from = lax.rem(c - 2 + 4 * odd + nc, nc)
    strip = (1, 2 - 2 * odd, 2 * odd)

    barrier = pltpu.get_barrier_semaphore()
    partners = [{"col": near_col}, {"col": far_col}, {"col": relay_from}]
    partners += [{"row": flip(r, 1 << k)} for k in range(bits)]
    for partner in partners:
        pl.semaphore_signal(barrier, inc=1, device_id=partner, device_id_type=MESH)
    pl.semaphore_wait(barrier, len(partners))

    piece = samples // CHUNKS

    def near_copy(k):
        rows = pl.ds(k * piece, piece)
        return pltpu.make_async_remote_copy(
            obs.at[rows], near.at[rows], near_send.at[k], near_recv.at[k],
            device_id={"col": near_col}, device_id_type=MESH,
        )

    def far_copy(k):
        rows = pl.ds(k * piece, piece)
        return pltpu.make_async_remote_copy(
            near.at[rows], far.at[rows], far_send.at[k], far_recv.at[k],
            device_id={"col": relay_to}, device_id_type=MESH,
        )

    near_copies = [near_copy(k) for k in range(CHUNKS)]
    far_copies = [far_copy(k) for k in range(CHUNKS)]
    for copy in near_copies:
        copy.start()

    def relay(k):
        near_copies[k].wait_recv()
        far_copies[k].start()

    def convert(source, kind, h):
        rows = pl.ds(h * HALF, HALF)
        for a in range(TB):
            block = source[rows, pl.ds(a * BLK, BLK)]
            high, low = split(block)
            xs[kind * TB + a, rows, :] = jnp.concatenate([high, low], axis=1)
            high, low = split(block.T)
            xt[kind * TB + a, :, rows] = jnp.concatenate([high, low], axis=0)

    def entry(kind, at):
        return tab[strip[kind], at]

    def weights(kind):
        def body(at, _):
            slot = entry(kind, at)
            live = entry(kind, 2 * kmax + slot) >= 0
            high, low = split(jnp.where(live, omega[0, strip[kind], slot], 0.0))
            top = jnp.concatenate([high, low], axis=1)
            bottom = jnp.concatenate([high, jnp.zeros_like(low)], axis=1)
            wcat[kind * kmax + at] = jnp.concatenate([top, bottom], axis=0)
            return 0

        lax.fori_loop(0, kmax, body, 0, unroll=2)
        cum[kind * (kmax + 1) + kmax] = jnp.zeros((samples, BLK), f32)

    def products(kind, h):
        rows = pl.ds(h * HALF, HALF)

        def body(at, total):
            slot = entry(kind, at)
            keep = entry(kind, kmax + at).astype(f32)
            a = lax.div(jnp.maximum(entry(kind, 2 * kmax + slot), 0), TB)
            both = jnp.dot(
                xs[kind * TB + a, rows, :], wcat[kind * kmax + at], preferred_element_type=f32
            )
            total = total * keep + (both[:, :BLK] + both[:, BLK:])
            cum[kind * (kmax + 1) + at, rows, :] = total
            return total

        lax.fori_loop(0, kmax, body, jnp.zeros((HALF, BLK), f32), unroll=4)

    halves = samples // HALF
    per_half = CHUNKS // halves

    def own_work():
        for h in range(halves):
            yield lambda h=h: convert(obs, 0, h)
        yield lambda: weights(0)
        for h in range(halves):
            yield lambda h=h: products(0, h)
        yield lambda: weights(1)
        yield lambda: weights(2)

    for k, work in enumerate(own_work()):
        work()
        if k < CHUNKS:
            relay(k)
    done = min(k + 1, CHUNKS)
    for h in range(halves):
        while done < (h + 1) * per_half:
            relay(done)
            done += 1
        convert(near, 1, h)
        if done < CHUNKS:
            relay(done)
            done += 1
        products(1, h)
        for k in range(h * per_half, (h + 1) * per_half):
            far_copies[k].wait_recv()
        convert(far, 2, h)
        products(2, h)
    for copy in near_copies + far_copies:
        copy.wait_send()

    def collect(b, _):
        total = cum[entry(0, 3 * kmax + b)]
        for kind in (1, 2):
            total = total + cum[kind * (kmax + 1) + entry(kind, 3 * kmax + b)]
        high, low = split(total)
        rs[b] = jnp.concatenate([high, low], axis=1)
        return 0

    lax.fori_loop(0, TB, collect, 0, unroll=2)

    def forward(kind, slot):
        place = jnp.maximum(entry(kind, 2 * kmax + slot), 0)
        both = jnp.dot(
            xt[kind * TB + lax.div(place, TB)], rs[lax.rem(place, TB)], preferred_element_type=f32
        )
        both = both[:BLK] + both[BLK:]
        return both[:, :BLK] + both[:, BLK:]

    def mate(slot):
        return slot + lax.div(slot, TB) * (1 - 2 * lax.rem(slot, 2))

    paired_here = share % 2 == 0

    def row_copy(kind, q):
        bit = q & -q
        return pltpu.make_async_remote_copy(
            fbuf.at[kind, q], rbuf.at[kind, q - 1], row_send.at[kind, q - 1],
            row_recv.at[kind, q - 1], device_id={"row": flip(r, bit)}, device_id_type=MESH,
        )

    row_copies = {(kind, q): row_copy(kind, q) for kind in range(3) for q in range(1, nr)}

    def group(kind, q):
        first = flip(r, q) * share

        def body(s, _):
            part = forward(kind, first + s)
            if kind == 0 and not paired_here:
                part = part + forward(kind, mate(first + s)).T
            fbuf[kind, q, s] = part
            return 0

        lax.fori_loop(0, share, body, 0, unroll=True)

    def add_arrived(kind, q, bit):
        row_copies[kind, q | bit].wait_recv()
        fbuf[kind, q] = fbuf[kind, q] + rbuf[kind, (q | bit) - 1]

    def reduce(kind, q):
        group(kind, q)
        low = q & -q if q else nr // 2
        bit = 1
        while bit < low:
            add_arrived(kind, q, bit)
            bit *= 2
        if q:
            row_copies[kind, q].start()

    order = (1, 2, 0)
    for kind in order:
        for q in range(nr - 1, nr // 2 - 1, -1):
            reduce(kind, q)
    for kind in order:
        for q in range(nr // 2 - 1, -1, -1):
            reduce(kind, q)

    mirrors = {
        kind: pltpu.make_async_remote_copy(
            fbuf.at[kind, 0], mrecv.at[kind - 1], mir_send.at[kind - 1], mir_recv.at[kind - 1],
            device_id={"col": near_col if kind == 1 else far_col}, device_id_type=MESH,
        )
        for kind in (1, 2)
    }
    scale = 0.5 / (samples * nr)
    eye = lax.broadcasted_iota(jnp.int32, (BLK, BLK), 0) == lax.broadcasted_iota(jnp.int32, (BLK, BLK), 1)

    def finish(kind, s, mirrored):
        slot = r * share + s
        place = entry(kind, 2 * kmax + slot)
        gradient = fbuf[kind, 0, s] * scale if mirrored is None else (fbuf[kind, 0, s] + mirrored) * scale
        old = omega[0, strip[kind], slot]
        edge = step_size * penalty
        if kind == 0:
            on_diagonal = eye & (lax.div(place, TB) == lax.rem(place, TB)) & (place >= 0)
            inverse = jnp.where(on_diagonal, 1.0 / jnp.where(on_diagonal, old, 1.0), 0.0)
            gradient = gradient - inverse
        trial = old - step_size * gradient
        shrunk = jnp.where(trial > edge, trial - edge, jnp.where(trial < -edge, trial + edge, 0.0))
        if kind == 0:
            shrunk = jnp.where(on_diagonal, trial, shrunk)
        out[0, strip[kind], s] = jnp.where(place >= 0, shrunk, 0.0)

    for kind in order:
        if nr > 1:
            add_arrived(kind, 0, nr // 2)
        if kind:
            mirrors[kind].start()
    for s in range(share):
        if paired_here:
            other = s + lax.div(r * share, TB) * (1 - 2 * (s % 2))
            finish(0, s, fbuf[0, 0, other].T)
        else:
            finish(0, s, None)
    for kind in (1, 2):
        mirrors[kind].wait_recv()
        for s in range(share):
            finish(kind, s, mrecv[kind - 1, s].T)
    for copy in row_copies.values():
        copy.wait_send()
    for copy in mirrors.values():
        copy.wait_send()


def tables(slots):
    kmax = slots.shape[1]
    column = jnp.where(slots >= 0, slots % TB, TB)
    index = jnp.arange(kmax, dtype=jnp.int32)
    mine, other = column[:, :, None], column[:, None, :]
    ahead = (other < mine) | ((other == mine) & (index[None, :] < index[:, None]))
    rank = jnp.sum(ahead.astype(jnp.int32), axis=2)
    at = (rank[:, None, :] == index[:, None]).astype(jnp.int32)
    order = jnp.sum(at * index, axis=2)
    before = jnp.sum(((other == mine) & (index[None, :] < index[:, None])).astype(jnp.int32), axis=2)
    keep = jnp.sum(at * (before > 0).astype(jnp.int32)[:, None, :], axis=2)
    wanted = jnp.arange(TB, dtype=jnp.int32)[None, :, None]
    upto = jnp.sum((column[:, None, :] <= wanted).astype(jnp.int32), axis=2)
    within = jnp.sum((column[:, None, :] == wanted).astype(jnp.int32), axis=2)
    last = jnp.where(within > 0, upto - 1, kmax)
    return jnp.concatenate([order, keep, slots, last], axis=1).astype(jnp.int32)


def solution(mesh):
    nr, nc = mesh.shape["row"], mesh.shape["col"]

    def on_device(observations, omega, block_slots):
        samples, width = observations.shape
        kmax = omega.shape[2]
        share = kmax // nr
        vmem = pl.BlockSpec(memory_space=pltpu.VMEM)
        dma = pltpu.SemaphoreType.DMA
        return pl.pallas_call(
            functools.partial(kernel, nr, nc, kmax),
            out_shape=jax.ShapeDtypeStruct((1, 3, share, BLK, BLK), f32),
            in_specs=[pl.BlockSpec(memory_space=pltpu.SMEM), vmem, vmem],
            out_specs=vmem,
            scratch_shapes=[
                pltpu.VMEM((samples, width), f32),
                pltpu.VMEM((samples, width), f32),
                pltpu.VMEM((3 * TB, samples, 2 * BLK), bf16),
                pltpu.VMEM((3 * TB, 2 * BLK, samples), bf16),
                pltpu.VMEM((3 * kmax, 2 * BLK, 2 * BLK), bf16),
                pltpu.VMEM((3 * (kmax + 1), samples, BLK), f32),
                pltpu.VMEM((TB, samples, 2 * BLK), bf16),
                pltpu.VMEM((3, nr, share, BLK, BLK), f32),
                pltpu.VMEM((3, nr - 1, share, BLK, BLK), f32),
                pltpu.VMEM((2, share, BLK, BLK), f32),
                dma((CHUNKS,)),
                dma((CHUNKS,)),
                dma((CHUNKS,)),
                dma((CHUNKS,)),
                dma((3, nr - 1)),
                dma((3, nr - 1)),
                dma((2,)),
                dma((2,)),
            ],
            compiler_params=pltpu.CompilerParams(
                collective_id=0, has_side_effects=True, vmem_limit_bytes=56 * 1024 * 1024
            ),
        )(tables(block_slots[0]), observations, omega)

    return jax.shard_map(
        on_device,
        mesh=mesh,
        in_specs=(P("row", "col"), P("col", None, None, None, None), P("col", None, None)),
        out_specs=P("col", None, "row", None, None),
        check_vma=False,
    )
```

time: 237 us -> 69.7 us (0.29)
  waiting for transfers between devices: 121 us -> 0 us
  Pallas kernels: 0 us -> 64.7 us
  local copies, waits for them, and re-layouts: 41.9 us -> 2.74 us
  matrix products: 37.5 us -> 0 us
  between operations: 14.1 us -> 0.02 us
  other arithmetic: 12.1 us -> 1.99 us
  starting transfers between devices: 9.54 us -> 0 us
    ppermute x4 -> x0, waiting for transfers between devices: 76.3 us -> none  [shifted(): return lax.ppermute(value, axis, pairs)]
    pallas_call x0 -> x1, Pallas kernels: none -> 64.7 us  [on_device(): pl.pallas_call(functools.partial(kernel, nr, nc, kmax), out_shape=jax.Sha...]
    unnamed x2 -> x0, waiting for transfers between devices: 44.5 us -> none
    dot_general x6 -> x0, matrix products: 37.5 us -> none  [the longest x1 13.2 us: local_terms(): jnp.einsum('ejpk,ejkl->ejpl', chosen, omega_strip, precision=highest)]
    dynamic_slice x3 -> x0, local copies, waits for them, and re-layouts: 18.5 us -> none  [the longest x2 18.4 us: on_device(): lax.dynamic_slice_in_dim(omega_strip, first_slot, share_slots, 1)]
    ppermute x4 -> x0, starting transfers between devices: 9.54 us -> none  [shifted(): return lax.ppermute(value, axis, pairs)]
    dot_general x2 -> x0, local copies, waits for them, and re-layouts: 9.4 us -> none  [the longest x1 6.84 us: local_terms(): chosen = jnp.einsum('ejn,epnk->ejpk', row_pick, nearby, precision=highest)]
    another operation x3 -> x0, other arithmetic: 4.99 us -> none  [on_device(): jnp.stack([0.5 * (forward[0] + jnp.swapaxes(left_part, 1, 2)), inner_half...]
  transfers between devices with their start and end apart: 5 -> 0, of which waited for: 4 -> 0; matrix products, arithmetic and copies ran while one was open for 17% -> 0% of each run, Pallas kernels for 0% -> 0%
where the time goes in v1:
time: 69.7 us; the launch traced here: 69.5 us
  Pallas kernels  64.7 us (93%)
  local copies, waits for them, and re-layouts  2.74 us (4%)
  other arithmetic  1.99 us (3%)
    pallas_call x1, Pallas kernels, on_device(): pl.pallas_call(functools.partial(kernel, nr, nc, kmax), out_shape=jax.Sha...  64.7 us
    unnamed x2, local copies, waits for them, and re-layouts  2.74 us

profile of v1, /device:TPU:0, one launch (start us, length us, event | category | flops | bytes accessed | tf_op | source)
XLA Modules:
  0.0 69.5 jit_solution(6167546812143068771)
XLA Ops:
  0.0 0.7 fusion.1
  0.7 0.7 copy.8
  1.4 0.3 convert_reduce_fusion.1
  1.6 0.2 select_reduce_fusion.1
  1.8 0.2 convert_reduce_fusion.3
  2.0 0.7 pad_add_fusion.tab
  2.7 64.7 %shard_map.37 = f32[1,3,4,128,128]{4,3,2,1,0:T(8,128)} custom-call(s32[3,56]{1,0:T(4,128)} %pad_add_fusion.tab, f32[256,1024]{1,0:T(8,128)} %obs.1, f32[1,3,16,128,128]{4,3,2,1,0:T(8,128)} %omega.1), custom_call_target="tpu_custom_call" | custom-call | tf_op jit(solution)/shard_map/pallas_call | solution.py:296
  67.4 2.1 %copy.10 = f32[1,3,4,128,128]{4,3,2,1,0:T(8,128)} copy(f32[1,3,4,128,128]{4,3,2,1,0:T(8,128)} %shard_map.37) | data formatting | bytes 1572864
  (3 shorter events, 0.0 us)

commit v2 on v1

--- a/solution.py
+++ b/solution.py
@@ -10,8 +10,8 @@
 MESH = pl.DeviceIdType.MESH
 BLK = 128
 TB = 8
-HALF = 128
-CHUNKS = 8
+CHUNKS = 16
+WINDOW = 4
 
 step_size = 0.5
 penalty = 0.1
@@ -33,10 +33,12 @@
 
 
 def kernel(
-    nr, nc, kmax, tab, obs, omega, out, near, far, xs, xt, wcat, cum, rs, fbuf, rbuf, mrecv,
-    near_send, near_recv, far_send, far_recv, row_send, row_recv, mir_send, mir_recv,
+    nr, nc, kmax, slots, obs_in, omega_in, out, tab, obs, omega, near, far, xs, xt, wcat, cum, rs, fbuf, rbuf,
+    mrecv, load, near_send, near_recv, far_send, far_recv, row_send, row_recv, mir_send, mir_recv,
 ):
-    samples = obs.shape[0]
+    samples = obs_in.shape[0]
+    load_obs = pltpu.make_async_copy(obs_in, obs, load.at[0])
+    load_omega = pltpu.make_async_copy(omega_in, omega, load.at[1])
     share = kmax // nr
     bits = nr.bit_length() - 1
     r, c = lax.axis_index("row"), lax.axis_index("col")
@@ -59,7 +61,7 @@
     def near_copy(k):
         rows = pl.ds(k * piece, piece)
         return pltpu.make_async_remote_copy(
-            obs.at[rows], near.at[rows], near_send.at[k], near_recv.at[k],
+            obs_in.at[rows], near.at[rows], near_send.at[k], near_recv.at[k],
             device_id={"col": near_col}, device_id_type=MESH,
         )
 
@@ -72,15 +74,20 @@
 
     near_copies = [near_copy(k) for k in range(CHUNKS)]
     far_copies = [far_copy(k) for k in range(CHUNKS)]
-    for copy in near_copies:
+    for copy in near_copies[:WINDOW]:
         copy.start()
+    load_obs.start()
+    load_omega.start()
 
     def relay(k):
         near_copies[k].wait_recv()
         far_copies[k].start()
-
-    def convert(source, kind, h):
-        rows = pl.ds(h * HALF, HALF)
+        near_copies[k].wait_send()
+        if k + WINDOW < CHUNKS:
+            near_copies[k + WINDOW].start()
+
+    def convert(source, kind, first, count):
+        rows = pl.ds(first, count)
         for a in range(TB):
             block = source[rows, pl.ds(a * BLK, BLK)]
             high, low = split(block)
@@ -88,75 +95,103 @@
             high, low = split(block.T)
             xt[kind * TB + a, :, rows] = jnp.concatenate([high, low], axis=0)
 
+    def fill(e, _):
+        places = [slots[e, 0, j] for j in range(kmax)]
+        columns = [jnp.where(p >= 0, lax.rem(jnp.maximum(p, 0), TB), TB) for p in places]
+        for j in range(kmax):
+            before = jnp.int32(kmax)
+            for i in range(j):
+                before = jnp.where(columns[i] == columns[j], i, before)
+            tab[e, j] = before
+        for b in range(TB):
+            last = jnp.int32(kmax)
+            for j in range(kmax):
+                last = jnp.where(columns[j] == b, j, last)
+            tab[e, kmax + b] = last
+        return 0
+
     def entry(kind, at):
         return tab[strip[kind], at]
 
+    def position(kind, slot):
+        return slots[strip[kind], 0, slot]
+
     def weights(kind):
-        def body(at, _):
-            slot = entry(kind, at)
-            live = entry(kind, 2 * kmax + slot) >= 0
+        def body(slot, _):
+            live = position(kind, slot) >= 0
             high, low = split(jnp.where(live, omega[0, strip[kind], slot], 0.0))
             top = jnp.concatenate([high, low], axis=1)
             bottom = jnp.concatenate([high, jnp.zeros_like(low)], axis=1)
-            wcat[kind * kmax + at] = jnp.concatenate([top, bottom], axis=0)
+            wcat[kind * kmax + slot] = jnp.concatenate([top, bottom], axis=0)
             return 0
 
         lax.fori_loop(0, kmax, body, 0, unroll=2)
         cum[kind * (kmax + 1) + kmax] = jnp.zeros((samples, BLK), f32)
 
-    def products(kind, h):
-        rows = pl.ds(h * HALF, HALF)
-
-        def body(at, total):
-            slot = entry(kind, at)
-            keep = entry(kind, kmax + at).astype(f32)
-            a = lax.div(jnp.maximum(entry(kind, 2 * kmax + slot), 0), TB)
+    def products(kind, first, count):
+        rows = pl.ds(first, count)
+
+        def body(slot, _):
+            a = lax.div(jnp.maximum(position(kind, slot), 0), TB)
             both = jnp.dot(
-                xs[kind * TB + a, rows, :], wcat[kind * kmax + at], preferred_element_type=f32
+                xs[kind * TB + a, rows, :], wcat[kind * kmax + slot], preferred_element_type=f32
             )
-            total = total * keep + (both[:, :BLK] + both[:, BLK:])
-            cum[kind * (kmax + 1) + at, rows, :] = total
-            return total
-
-        lax.fori_loop(0, kmax, body, jnp.zeros((HALF, BLK), f32), unroll=4)
-
-    halves = samples // HALF
-    per_half = CHUNKS // halves
-
-    def own_work():
-        for h in range(halves):
-            yield lambda h=h: convert(obs, 0, h)
-        yield lambda: weights(0)
-        for h in range(halves):
-            yield lambda h=h: products(0, h)
-        yield lambda: weights(1)
-        yield lambda: weights(2)
-
-    for k, work in enumerate(own_work()):
-        work()
-        if k < CHUNKS:
-            relay(k)
-    done = min(k + 1, CHUNKS)
-    for h in range(halves):
-        while done < (h + 1) * per_half:
+            before = cum[kind * (kmax + 1) + entry(kind, slot), rows, :]
+            cum[kind * (kmax + 1) + slot, rows, :] = before + (both[:, :BLK] + both[:, BLK:])
+            return 0
+
+        lax.fori_loop(0, kmax, body, 0, unroll=4)
+
+    piece_rows = samples // CHUNKS
+    half, quarter = samples // 2, samples // 4
+    done = 0
+
+    def relay_to_row(row):
+        nonlocal done
+        while done < row // piece_rows:
             relay(done)
             done += 1
-        convert(near, 1, h)
+
+    def relay_next():
+        nonlocal done
         if done < CHUNKS:
             relay(done)
             done += 1
-        products(1, h)
-        for k in range(h * per_half, (h + 1) * per_half):
+
+    lax.fori_loop(0, 3, fill, 0)
+    load_obs.wait()
+    convert(obs, 0, 0, half)
+    relay_next()
+    convert(obs, 0, half, half)
+    relay_next()
+    load_omega.wait()
+    weights(0)
+    relay_next()
+    products(0, 0, half)
+    relay_next()
+    products(0, half, half)
+    relay_next()
+    weights(1)
+    relay_next()
+    weights(2)
+    for first, count in ((0, half), (half, quarter), (half + quarter, quarter)):
+        relay_to_row(first + count)
+        convert(near, 1, first, count)
+        relay_next()
+        products(1, first, count)
+        relay_next()
+        for k in range(first // piece_rows, (first + count) // piece_rows):
             far_copies[k].wait_recv()
-        convert(far, 2, h)
-        products(2, h)
-    for copy in near_copies + far_copies:
+        convert(far, 2, first, count)
+        relay_next()
+        products(2, first, count)
+    for copy in far_copies:
         copy.wait_send()
 
     def collect(b, _):
-        total = cum[entry(0, 3 * kmax + b)]
+        total = cum[entry(0, kmax + b)]
         for kind in (1, 2):
-            total = total + cum[kind * (kmax + 1) + entry(kind, 3 * kmax + b)]
+            total = total + cum[kind * (kmax + 1) + entry(kind, kmax + b)]
         high, low = split(total)
         rs[b] = jnp.concatenate([high, low], axis=1)
         return 0
@@ -164,7 +199,7 @@
     lax.fori_loop(0, TB, collect, 0, unroll=2)
 
     def forward(kind, slot):
-        place = jnp.maximum(entry(kind, 2 * kmax + slot), 0)
+        place = jnp.maximum(position(kind, slot), 0)
         both = jnp.dot(
             xt[kind * TB + lax.div(place, TB)], rs[lax.rem(place, TB)], preferred_element_type=f32
         )
@@ -211,7 +246,7 @@
         if q:
             row_copies[kind, q].start()
 
-    order = (1, 2, 0)
+    order = (2, 1, 0)
     for kind in order:
         for q in range(nr - 1, nr // 2 - 1, -1):
             reduce(kind, q)
@@ -231,7 +266,7 @@
 
     def finish(kind, s, mirrored):
         slot = r * share + s
-        place = entry(kind, 2 * kmax + slot)
+        place = position(kind, slot)
         gradient = fbuf[kind, 0, s] * scale if mirrored is None else (fbuf[kind, 0, s] + mirrored) * scale
         old = omega[0, strip[kind], slot]
         edge = step_size * penalty
@@ -245,45 +280,29 @@
             shrunk = jnp.where(on_diagonal, trial, shrunk)
         out[0, strip[kind], s] = jnp.where(place >= 0, shrunk, 0.0)
 
-    for kind in order:
-        if nr > 1:
-            add_arrived(kind, 0, nr // 2)
-        if kind:
-            mirrors[kind].start()
+    def finish_outer(kind):
+        mirrors[kind].wait_recv()
+        for s in range(share):
+            finish(kind, s, mrecv[kind - 1, s].T)
+
+    for kind in (2, 1):
+        add_arrived(kind, 0, nr // 2)
+        mirrors[kind].start()
+    finish_outer(2)
+    add_arrived(0, 0, nr // 2)
     for s in range(share):
         if paired_here:
             other = s + lax.div(r * share, TB) * (1 - 2 * (s % 2))
             finish(0, s, fbuf[0, 0, other].T)
         else:
             finish(0, s, None)
-    for kind in (1, 2):
-        mirrors[kind].wait_recv()
-        for s in range(share):
-            finish(kind, s, mrecv[kind - 1, s].T)
+    finish_outer(1)
     for copy in row_copies.values():
         copy.wait_send()
     for copy in mirrors.values():
         copy.wait_send()
 
 
-def tables(slots):
-    kmax = slots.shape[1]
-    column = jnp.where(slots >= 0, slots % TB, TB)
-    index = jnp.arange(kmax, dtype=jnp.int32)
-    mine, other = column[:, :, None], column[:, None, :]
-    ahead = (other < mine) | ((other == mine) & (index[None, :] < index[:, None]))
-    rank = jnp.sum(ahead.astype(jnp.int32), axis=2)
-    at = (rank[:, None, :] == index[:, None]).astype(jnp.int32)
-    order = jnp.sum(at * index, axis=2)
-    before = jnp.sum(((other == mine) & (index[None, :] < index[:, None])).astype(jnp.int32), axis=2)
-    keep = jnp.sum(at * (before > 0).astype(jnp.int32)[:, None, :], axis=2)
-    wanted = jnp.arange(TB, dtype=jnp.int32)[None, :, None]
-    upto = jnp.sum((column[:, None, :] <= wanted).astype(jnp.int32), axis=2)
-    within = jnp.sum((column[:, None, :] == wanted).astype(jnp.int32), axis=2)
-    last = jnp.where(within > 0, upto - 1, kmax)
-    return jnp.concatenate([order, keep, slots, last], axis=1).astype(jnp.int32)
-
-
 def solution(mesh):
     nr, nc = mesh.shape["row"], mesh.shape["col"]
 
@@ -291,14 +310,17 @@
         samples, width = observations.shape
         kmax = omega.shape[2]
         share = kmax // nr
-        vmem = pl.BlockSpec(memory_space=pltpu.VMEM)
+        vmem, here = pl.BlockSpec(memory_space=pltpu.VMEM), pl.BlockSpec(memory_space=pltpu.HBM)
         dma = pltpu.SemaphoreType.DMA
         return pl.pallas_call(
             functools.partial(kernel, nr, nc, kmax),
             out_shape=jax.ShapeDtypeStruct((1, 3, share, BLK, BLK), f32),
-            in_specs=[pl.BlockSpec(memory_space=pltpu.SMEM), vmem, vmem],
+            in_specs=[pl.BlockSpec(memory_space=pltpu.SMEM), here, here],
             out_specs=vmem,
             scratch_shapes=[
+                pltpu.SMEM((3, kmax + TB), jnp.int32),
+                pltpu.VMEM((samples, width), f32),
+                pltpu.VMEM(omega.shape, f32),
                 pltpu.VMEM((samples, width), f32),
                 pltpu.VMEM((samples, width), f32),
                 pltpu.VMEM((3 * TB, samples, 2 * BLK), bf16),
@@ -309,6 +331,7 @@
                 pltpu.VMEM((3, nr, share, BLK, BLK), f32),
                 pltpu.VMEM((3, nr - 1, share, BLK, BLK), f32),
                 pltpu.VMEM((2, share, BLK, BLK), f32),
+                dma((2,)),
                 dma((CHUNKS,)),
                 dma((CHUNKS,)),
                 dma((CHUNKS,)),
@@ -319,9 +342,9 @@
                 dma((2,)),
             ],
             compiler_params=pltpu.CompilerParams(
-                collective_id=0, has_side_effects=True, vmem_limit_bytes=56 * 1024 * 1024
+                collective_id=0, has_side_effects=True, vmem_limit_bytes=40 * 1024 * 1024
             ),
-        )(tables(block_slots[0]), observations, omega)
+        )(jnp.transpose(block_slots, (1, 0, 2)), observations, omega)
 
     return jax.shard_map(
         on_device,

time: 69.7 us -> 66.8 us (0.958)
  Pallas kernels: 64.7 us -> 61.9 us
  other arithmetic: 1.99 us -> 0 us
  local copies, waits for them, and re-layouts: 2.74 us -> 4.68 us
    pallas_call x1, Pallas kernels: 64.7 us -> 61.9 us  [on_device(): pl.pallas_call(functools.partial(kernel, nr, nc, kmax), out_shape=jax.Sha...]
    unnamed x2 -> x7, local copies, waits for them, and re-layouts: 2.74 us -> 4.68 us
where the time goes in v2:
time: 66.8 us; the launch traced here: 66.6 us
  Pallas kernels  61.9 us (93%)
  local copies, waits for them, and re-layouts  4.68 us (7%)
    pallas_call x1, Pallas kernels, on_device(): pl.pallas_call(functools.partial(kernel, nr, nc, kmax), out_shape=jax.Sha...  61.9 us
    unnamed x7, local copies, waits for them, and re-layouts  4.68 us

profile of v2, /device:TPU:0, one launch (start us, length us, event | category | flops | bytes accessed | tf_op | source)
XLA Modules:
  0.0 66.6 jit_solution(15650694207789752190)
XLA Ops:
  0.0 0.0 copy-start
  0.0 1.9 %copy-done = f32[1,3,16,128,128]{4,3,2,1,0:T(8,128)S(1)} copy-done((f32[1,3,16,128,128]{4,3,2,1,0:T(8,128)S(1)}, f32[1,3,16,128,128]{4,3,2,1,0:T(8,128)}, u32[]{:S(2)}) %copy-start) | copy-done | bytes 3145752
  1.9 0.0 copy-start.1
  1.9 1.2 %copy-done.1 = f32[256,1024]{1,0:T(8,128)S(1)} copy-done((f32[256,1024]{1,0:T(8,128)S(1)}, f32[256,1024]{1,0:T(8,128)}, u32[]{:S(2)}) %copy-start.1) | copy-done | bytes 1048600
  3.1 0.0 copy-start.2
  3.1 0.7 %copy-done.2 = s32[1,3,16]{2,0,1:T(1,128)S(1)} copy-done((s32[1,3,16]{2,0,1:T(1,128)S(1)}, s32[1,3,16]{2,0,1:T(1,128)}, u32[]{:S(2)}) %copy-start.2) | copy-done | bytes 216
  3.8 61.9 %shard_map.37 = f32[1,3,4,128,128]{4,3,2,1,0:T(8,128)S(1)} custom-call(s32[3,1,16]{2,1,0:T(1,128)S(1)} %bitcast.1, f32[256,1024]{1,0:T(8,128)S(1)} %copy-done.1, f32[1,3,16,128,128]{4,3,2,1,0:T(8,128)S(1)} %copy-done), custom_call_target="tpu_custom_call" | custom-call | tf_op jit(solution)/shard_map/pallas_call | solution.py:315
  65.7 0.9 %copy.5 = f32[1,3,4,128,128]{4,3,2,1,0:T(8,128)} copy(f32[1,3,4,128,128]{4,3,2,1,0:T(8,128)S(1)} %shard_map.37) | data formatting | bytes 1572864
Async XLA Ops:
  0.0 1.9 %copy-start = (f32[1,3,16,128,128]{4,3,2,1,0:T(8,128)S(1)}, f32[1,3,16,128,128]{4,3,2,1,0:T(8,128)}, u32[]{:S(2)}) copy-start(f32[1,3,16,128,128]{4,3,2,1,0:T(8,128)} %omega_in.1) | copy-start | bytes 9437188
  1.9 1.2 %copy-start.1 = (f32[256,1024]{1,0:T(8,128)S(1)}, f32[256,1024]{1,0:T(8,128)}, u32[]{:S(2)}) copy-start(f32[256,1024]{1,0:T(8,128)} %obs_in.1) | copy-start | bytes 3145732
  3.1 0.7 %copy-start.2 = (s32[1,3,16]{2,0,1:T(1,128)S(1)}, s32[1,3,16]{2,0,1:T(1,128)}, u32[]{:S(2)}) copy-start(s32[1,3,16]{2,0,1:T(1,128)} %param.5) | copy-start | bytes 580

commit v3 on v2

--- a/solution.py
+++ b/solution.py
@@ -210,56 +210,66 @@
         return slot + lax.div(slot, TB) * (1 - 2 * lax.rem(slot, 2))
 
     paired_here = share % 2 == 0
-
-    def row_copy(kind, q):
+    parts = 2 if paired_here else 1
+    size = share // parts
+
+    def row_copy(kind, q, p):
         bit = q & -q
+        part = pl.ds(p * size, size)
         return pltpu.make_async_remote_copy(
-            fbuf.at[kind, q], rbuf.at[kind, q - 1], row_send.at[kind, q - 1],
-            row_recv.at[kind, q - 1], device_id={"row": flip(r, bit)}, device_id_type=MESH,
-        )
-
-    row_copies = {(kind, q): row_copy(kind, q) for kind in range(3) for q in range(1, nr)}
-
-    def group(kind, q):
+            fbuf.at[kind, q, part], rbuf.at[kind, q - 1, part], row_send.at[kind, q - 1, p],
+            row_recv.at[kind, q - 1, p], device_id={"row": flip(r, bit)}, device_id_type=MESH,
+        )
+
+    row_copies = {
+        (kind, q, p): row_copy(kind, q, p) for kind in range(3) for q in range(1, nr) for p in range(parts)
+    }
+
+    def group(kind, q, p):
         first = flip(r, q) * share
 
         def body(s, _):
-            part = forward(kind, first + s)
+            value = forward(kind, first + s)
             if kind == 0 and not paired_here:
-                part = part + forward(kind, mate(first + s)).T
-            fbuf[kind, q, s] = part
+                value = value + forward(kind, mate(first + s)).T
+            fbuf[kind, q, s] = value
             return 0
 
-        lax.fori_loop(0, share, body, 0, unroll=True)
-
-    def add_arrived(kind, q, bit):
-        row_copies[kind, q | bit].wait_recv()
-        fbuf[kind, q] = fbuf[kind, q] + rbuf[kind, (q | bit) - 1]
-
-    def reduce(kind, q):
-        group(kind, q)
+        lax.fori_loop(p * size, (p + 1) * size, body, 0, unroll=True)
+
+    def add_arrived(kind, q, bit, p):
+        row_copies[kind, q | bit, p].wait_recv()
+        part = pl.ds(p * size, size)
+        fbuf[kind, q, part] = fbuf[kind, q, part] + rbuf[kind, (q | bit) - 1, part]
+
+    def reduce(kind, q, p):
+        group(kind, q, p)
         low = q & -q if q else nr // 2
         bit = 1
         while bit < low:
-            add_arrived(kind, q, bit)
+            add_arrived(kind, q, bit, p)
             bit *= 2
         if q:
-            row_copies[kind, q].start()
+            row_copies[kind, q, p].start()
 
     order = (2, 1, 0)
     for kind in order:
-        for q in range(nr - 1, nr // 2 - 1, -1):
-            reduce(kind, q)
+        for p in range(parts):
+            for q in range(nr - 1, nr // 2 - 1, -1):
+                reduce(kind, q, p)
     for kind in order:
-        for q in range(nr // 2 - 1, -1, -1):
-            reduce(kind, q)
+        for p in range(parts):
+            for q in range(nr // 2 - 1, -1, -1):
+                reduce(kind, q, p)
 
     mirrors = {
-        kind: pltpu.make_async_remote_copy(
-            fbuf.at[kind, 0], mrecv.at[kind - 1], mir_send.at[kind - 1], mir_recv.at[kind - 1],
+        (kind, p): pltpu.make_async_remote_copy(
+            fbuf.at[kind, 0, pl.ds(p * size, size)], mrecv.at[kind - 1, pl.ds(p * size, size)],
+            mir_send.at[kind - 1, p], mir_recv.at[kind - 1, p],
             device_id={"col": near_col if kind == 1 else far_col}, device_id_type=MESH,
         )
         for kind in (1, 2)
+        for p in range(parts)
     }
     scale = 0.5 / (samples * nr)
     eye = lax.broadcasted_iota(jnp.int32, (BLK, BLK), 0) == lax.broadcasted_iota(jnp.int32, (BLK, BLK), 1)
@@ -281,15 +291,18 @@
         out[0, strip[kind], s] = jnp.where(place >= 0, shrunk, 0.0)
 
     def finish_outer(kind):
-        mirrors[kind].wait_recv()
-        for s in range(share):
-            finish(kind, s, mrecv[kind - 1, s].T)
+        for p in range(parts):
+            mirrors[kind, p].wait_recv()
+            for s in range(p * size, (p + 1) * size):
+                finish(kind, s, mrecv[kind - 1, s].T)
 
     for kind in (2, 1):
-        add_arrived(kind, 0, nr // 2)
-        mirrors[kind].start()
+        for p in range(parts):
+            add_arrived(kind, 0, nr // 2, p)
+            mirrors[kind, p].start()
     finish_outer(2)
-    add_arrived(0, 0, nr // 2)
+    for p in range(parts):
+        add_arrived(0, 0, nr // 2, p)
     for s in range(share):
         if paired_here:
             other = s + lax.div(r * share, TB) * (1 - 2 * (s % 2))
@@ -310,7 +323,8 @@
         samples, width = observations.shape
         kmax = omega.shape[2]
         share = kmax // nr
-        vmem, here = pl.BlockSpec(memory_space=pltpu.VMEM), pl.BlockSpec(memory_space=pltpu.HBM)
+        parts = 2 if share % 2 == 0 else 1
+        vmem, here = pl.BlockSpec(memory_space=pltpu.VMEM), pl.BlockSpec(memory_space=pl.ANY)
         dma = pltpu.SemaphoreType.DMA
         return pl.pallas_call(
             functools.partial(kernel, nr, nc, kmax),
@@ -336,13 +350,13 @@
                 dma((CHUNKS,)),
                 dma((CHUNKS,)),
                 dma((CHUNKS,)),
-                dma((3, nr - 1)),
-                dma((3, nr - 1)),
-                dma((2,)),
-                dma((2,)),
+                dma((3, nr - 1, parts)),
+                dma((3, nr - 1, parts)),
+                dma((2, parts)),
+                dma((2, parts)),
             ],
             compiler_params=pltpu.CompilerParams(
-                collective_id=0, has_side_effects=True, vmem_limit_bytes=40 * 1024 * 1024
+                collective_id=0, has_side_effects=True, vmem_limit_bytes=56 * 1024 * 1024
             ),
         )(jnp.transpose(block_slots, (1, 0, 2)), observations, omega)
 

time: 66.8 us -> 67.3 us (level)
  Pallas kernels: 61.9 us -> 65.1 us
  local copies, waits for them, and re-layouts: 4.68 us -> 2.06 us
    pallas_call x1, Pallas kernels: 61.9 us -> 65.1 us  [on_device(): pl.pallas_call(functools.partial(kernel, nr, nc, kmax), out_shape=jax.Sha...]
    unnamed x7 -> x1, local copies, waits for them, and re-layouts: 4.68 us -> 2.06 us
where the time goes in v3:
time: 67.3 us; the launch traced here: 67.2 us
  Pallas kernels  65.1 us (97%)
  local copies, waits for them, and re-layouts  2.06 us (3%)
    pallas_call x1, Pallas kernels, on_device(): pl.pallas_call(functools.partial(kernel, nr, nc, kmax), out_shape=jax.Sha...  65.1 us
    unnamed x1, local copies, waits for them, and re-layouts  2.06 us

profile of v3, /device:TPU:0, one launch (start us, length us, event | category | flops | bytes accessed | tf_op | source)
XLA Modules:
  0.0 67.2 jit_solution(7793450145840268272)
XLA Ops:
  0.0 65.1 %shard_map.37 = f32[1,3,4,128,128]{4,3,2,1,0:T(8,128)} custom-call(s32[3,1,16]{2,1,0:T(1,128)} %bitcast.1, f32[256,1024]{1,0:T(8,128)} %obs_in.1, f32[1,3,16,128,128]{4,3,2,1,0:T(8,128)} %omega_in.1), custom_call_target="tpu_custom_call" | custom-call | tf_op jit(solution)/shard_map/pallas_call | solution.py:329
  65.1 2.1 %copy.5 = f32[1,3,4,128,128]{4,3,2,1,0:T(8,128)} copy(f32[1,3,4,128,128]{4,3,2,1,0:T(8,128)} %shard_map.37) | data formatting | bytes 1572864

commit v4 on v2

--- a/solution.py
+++ b/solution.py
@@ -125,7 +125,7 @@
             wcat[kind * kmax + slot] = jnp.concatenate([top, bottom], axis=0)
             return 0
 
-        lax.fori_loop(0, kmax, body, 0, unroll=2)
+        lax.fori_loop(0, kmax, body, 0, unroll=4)
         cum[kind * (kmax + 1) + kmax] = jnp.zeros((samples, BLK), f32)
 
     def products(kind, first, count):
@@ -140,10 +140,10 @@
             cum[kind * (kmax + 1) + slot, rows, :] = before + (both[:, :BLK] + both[:, BLK:])
             return 0
 
-        lax.fori_loop(0, kmax, body, 0, unroll=4)
+        lax.fori_loop(0, kmax, body, 0, unroll=8)
 
     piece_rows = samples // CHUNKS
-    half, quarter = samples // 2, samples // 4
+    half = samples // 2
     done = 0
 
     def relay_to_row(row):
@@ -167,14 +167,13 @@
     load_omega.wait()
     weights(0)
     relay_next()
-    products(0, 0, half)
-    relay_next()
-    products(0, half, half)
+    products(0, 0, samples)
+    relay_next()
     relay_next()
     weights(1)
     relay_next()
     weights(2)
-    for first, count in ((0, half), (half, quarter), (half + quarter, quarter)):
+    for first, count in ((0, half), (half, half)):
         relay_to_row(first + count)
         convert(near, 1, first, count)
         relay_next()
@@ -196,7 +195,7 @@
         rs[b] = jnp.concatenate([high, low], axis=1)
         return 0
 
-    lax.fori_loop(0, TB, collect, 0, unroll=2)
+    lax.fori_loop(0, TB, collect, 0, unroll=4)
 
     def forward(kind, slot):
         place = jnp.maximum(position(kind, slot), 0)
@@ -310,7 +309,7 @@
         samples, width = observations.shape
         kmax = omega.shape[2]
         share = kmax // nr
-        vmem, here = pl.BlockSpec(memory_space=pltpu.VMEM), pl.BlockSpec(memory_space=pltpu.HBM)
+        vmem, here = pl.BlockSpec(memory_space=pltpu.VMEM), pl.BlockSpec(memory_space=pl.ANY)
         dma = pltpu.SemaphoreType.DMA
         return pl.pallas_call(
             functools.partial(kernel, nr, nc, kmax),
@@ -342,7 +341,7 @@
                 dma((2,)),
             ],
             compiler_params=pltpu.CompilerParams(
-                collective_id=0, has_side_effects=True, vmem_limit_bytes=40 * 1024 * 1024
+                collective_id=0, has_side_effects=True, vmem_limit_bytes=56 * 1024 * 1024
             ),
         )(jnp.transpose(block_slots, (1, 0, 2)), observations, omega)
 

time: 66.8 us -> 64.8 us (0.970)
  local copies, waits for them, and re-layouts: 4.68 us -> 2.06 us
  Pallas kernels: 61.9 us -> 62.6 us
    unnamed x7 -> x1, local copies, waits for them, and re-layouts: 4.68 us -> 2.06 us
where the time goes in v4:
time: 64.8 us; the launch traced here: 64.7 us
  Pallas kernels  62.6 us (97%)
  local copies, waits for them, and re-layouts  2.06 us (3%)
    pallas_call x1, Pallas kernels, on_device(): pl.pallas_call(functools.partial(kernel, nr, nc, kmax), out_shape=jax.Sha...  62.6 us
    unnamed x1, local copies, waits for them, and re-layouts  2.06 us

profile of v4, /device:TPU:0, one launch (start us, length us, event | category | flops | bytes accessed | tf_op | source)
XLA Modules:
  0.0 64.7 jit_solution(15514016218289331288)
XLA Ops:
  0.0 62.6 %shard_map.37 = f32[1,3,4,128,128]{4,3,2,1,0:T(8,128)} custom-call(s32[3,1,16]{2,1,0:T(1,128)} %bitcast.1, f32[256,1024]{1,0:T(8,128)} %obs_in.1, f32[1,3,16,128,128]{4,3,2,1,0:T(8,128)} %omega_in.1), custom_call_target="tpu_custom_call" | custom-call | tf_op jit(solution)/shard_map/pallas_call | solution.py:314
  62.6 2.1 %copy.5 = f32[1,3,4,128,128]{4,3,2,1,0:T(8,128)} copy(f32[1,3,4,128,128]{4,3,2,1,0:T(8,128)} %shard_map.37) | data formatting | bytes 1572864

commit v5 on v4

--- a/solution.py
+++ b/solution.py
@@ -11,6 +11,7 @@
 BLK = 128
 TB = 8
 CHUNKS = 16
+STEP = 4
 WINDOW = 4
 
 step_size = 0.5
@@ -117,30 +118,40 @@
         return slots[strip[kind], 0, slot]
 
     def weights(kind):
-        def body(slot, _):
-            live = position(kind, slot) >= 0
-            high, low = split(jnp.where(live, omega[0, strip[kind], slot], 0.0))
-            top = jnp.concatenate([high, low], axis=1)
-            bottom = jnp.concatenate([high, jnp.zeros_like(low)], axis=1)
-            wcat[kind * kmax + slot] = jnp.concatenate([top, bottom], axis=0)
+        def body(step, _):
+            built = []
+            for i in range(STEP):
+                slot = step * STEP + i
+                live = position(kind, slot) >= 0
+                built.append(split(jnp.where(live, omega[0, strip[kind], slot], 0.0)))
+            for i, (high, low) in enumerate(built):
+                top = jnp.concatenate([high, low], axis=1)
+                bottom = jnp.concatenate([high, jnp.zeros_like(low)], axis=1)
+                wcat[kind * kmax + step * STEP + i] = jnp.concatenate([top, bottom], axis=0)
             return 0
 
-        lax.fori_loop(0, kmax, body, 0, unroll=4)
+        lax.fori_loop(0, kmax // STEP, body, 0)
         cum[kind * (kmax + 1) + kmax] = jnp.zeros((samples, BLK), f32)
 
     def products(kind, first, count):
         rows = pl.ds(first, count)
 
-        def body(slot, _):
-            a = lax.div(jnp.maximum(position(kind, slot), 0), TB)
-            both = jnp.dot(
-                xs[kind * TB + a, rows, :], wcat[kind * kmax + slot], preferred_element_type=f32
-            )
-            before = cum[kind * (kmax + 1) + entry(kind, slot), rows, :]
-            cum[kind * (kmax + 1) + slot, rows, :] = before + (both[:, :BLK] + both[:, BLK:])
+        def body(step, _):
+            made = []
+            for i in range(STEP):
+                slot = step * STEP + i
+                a = lax.div(jnp.maximum(position(kind, slot), 0), TB)
+                both = jnp.dot(
+                    xs[kind * TB + a, rows, :], wcat[kind * kmax + slot], preferred_element_type=f32
+                )
+                made.append(both[:, :BLK] + both[:, BLK:])
+            for i, value in enumerate(made):
+                slot = step * STEP + i
+                before = cum[kind * (kmax + 1) + entry(kind, slot), rows, :]
+                cum[kind * (kmax + 1) + slot, rows, :] = before + value
             return 0
 
-        lax.fori_loop(0, kmax, body, 0, unroll=8)
+        lax.fori_loop(0, kmax // STEP, body, 0, unroll=2)
 
     piece_rows = samples // CHUNKS
     half = samples // 2
@@ -167,7 +178,8 @@
     load_omega.wait()
     weights(0)
     relay_next()
-    products(0, 0, samples)
+    products(0, 0, half)
+    products(0, half, half)
     relay_next()
     relay_next()
     weights(1)
@@ -187,15 +199,18 @@
     for copy in far_copies:
         copy.wait_send()
 
-    def collect(b, _):
-        total = cum[entry(0, kmax + b)]
-        for kind in (1, 2):
-            total = total + cum[kind * (kmax + 1) + entry(kind, kmax + b)]
-        high, low = split(total)
-        rs[b] = jnp.concatenate([high, low], axis=1)
-        return 0
-
-    lax.fori_loop(0, TB, collect, 0, unroll=4)
+    for first in (0, half):
+        rows = pl.ds(first, half)
+        for start in range(0, TB, STEP):
+            sums = []
+            for b in range(start, start + STEP):
+                total = cum[entry(0, kmax + b), rows, :]
+                for kind in (1, 2):
+                    total = total + cum[kind * (kmax + 1) + entry(kind, kmax + b), rows, :]
+                sums.append(total)
+            for i, total in enumerate(sums):
+                high, low = split(total)
+                rs[start + i, rows, :] = jnp.concatenate([high, low], axis=1)
 
     def forward(kind, slot):
         place = jnp.maximum(position(kind, slot), 0)
@@ -222,14 +237,14 @@
     def group(kind, q):
         first = flip(r, q) * share
 
-        def body(s, _):
+        values = []
+        for s in range(share):
             part = forward(kind, first + s)
             if kind == 0 and not paired_here:
                 part = part + forward(kind, mate(first + s)).T
+            values.append(part)
+        for s, part in enumerate(values):
             fbuf[kind, q, s] = part
-            return 0
-
-        lax.fori_loop(0, share, body, 0, unroll=True)
 
     def add_arrived(kind, q, bit):
         row_copies[kind, q | bit].wait_recv()

time: 64.8 us -> 64.8 us (level)
  no operation moved by 1% of the time
where the time goes in v5:
time: 64.8 us; the launch traced here: 64.6 us
  Pallas kernels  62.6 us (97%)
  local copies, waits for them, and re-layouts  2.06 us (3%)
    pallas_call x1, Pallas kernels, on_device(): pl.pallas_call(functools.partial(kernel, nr, nc, kmax), out_shape=jax.Sha...  62.6 us
    unnamed x1, local copies, waits for them, and re-layouts  2.06 us

profile of v5, /device:TPU:0, one launch (start us, length us, event | category | flops | bytes accessed | tf_op | source)
XLA Modules:
  0.0 64.6 jit_solution(12655413018623855650)
XLA Ops:
  0.0 62.6 %shard_map.37 = f32[1,3,4,128,128]{4,3,2,1,0:T(8,128)} custom-call(s32[3,1,16]{2,1,0:T(1,128)} %bitcast.1, f32[256,1024]{1,0:T(8,128)} %obs_in.1, f32[1,3,16,128,128]{4,3,2,1,0:T(8,128)} %omega_in.1), custom_call_target="tpu_custom_call" | custom-call | tf_op jit(solution)/shard_map/pallas_call | solution.py:329
  62.6 2.1 %copy.5 = f32[1,3,4,128,128]{4,3,2,1,0:T(8,128)} copy(f32[1,3,4,128,128]{4,3,2,1,0:T(8,128)} %shard_map.37) | data formatting | bytes 1572864

commit v6 on v5

--- a/solution.py
+++ b/solution.py
@@ -55,6 +55,8 @@
     partners += [{"row": flip(r, 1 << k)} for k in range(bits)]
     for partner in partners:
         pl.semaphore_signal(barrier, inc=1, device_id=partner, device_id_type=MESH)
+    load_obs.start()
+    load_omega.start()
     pl.semaphore_wait(barrier, len(partners))
 
     piece = samples // CHUNKS
@@ -77,8 +79,6 @@
     far_copies = [far_copy(k) for k in range(CHUNKS)]
     for copy in near_copies[:WINDOW]:
         copy.start()
-    load_obs.start()
-    load_omega.start()
 
     def relay(k):
         near_copies[k].wait_recv()
@@ -185,7 +185,7 @@
     weights(1)
     relay_next()
     weights(2)
-    for first, count in ((0, half), (half, half)):
+    for first, count in ((0, half), (half, half // 2), (half + half // 2, half // 2)):
         relay_to_row(first + count)
         convert(near, 1, first, count)
         relay_next()
@@ -224,15 +224,23 @@
         return slot + lax.div(slot, TB) * (1 - 2 * lax.rem(slot, 2))
 
     paired_here = share % 2 == 0
-
-    def row_copy(kind, q):
+    parts = 2 if paired_here else 1
+    size = share // parts
+
+    def row_copy(kind, q, p):
         bit = q & -q
+        part = pl.ds(p * size, size) if bit == nr // 2 else pl.ds(0, share)
         return pltpu.make_async_remote_copy(
-            fbuf.at[kind, q], rbuf.at[kind, q - 1], row_send.at[kind, q - 1],
-            row_recv.at[kind, q - 1], device_id={"row": flip(r, bit)}, device_id_type=MESH,
-        )
-
-    row_copies = {(kind, q): row_copy(kind, q) for kind in range(3) for q in range(1, nr)}
+            fbuf.at[kind, q, part], rbuf.at[kind, q - 1, part], row_send.at[kind, q - 1, p],
+            row_recv.at[kind, q - 1, p], device_id={"row": flip(r, bit)}, device_id_type=MESH,
+        )
+
+    row_copies = {
+        (kind, q, p): row_copy(kind, q, p)
+        for kind in range(3)
+        for q in range(1, nr)
+        for p in range(parts if q == nr // 2 else 1)
+    }
 
     def group(kind, q):
         first = flip(r, q) * share
@@ -246,35 +254,53 @@
         for s, part in enumerate(values):
             fbuf[kind, q, s] = part
 
-    def add_arrived(kind, q, bit):
-        row_copies[kind, q | bit].wait_recv()
-        fbuf[kind, q] = fbuf[kind, q] + rbuf[kind, (q | bit) - 1]
-
-    def reduce(kind, q):
-        group(kind, q)
+    def settle(kind, q):
         low = q & -q if q else nr // 2
         bit = 1
         while bit < low:
-            add_arrived(kind, q, bit)
+            row_copies[kind, q | bit, 0].wait_recv()
+            fbuf[kind, q] = fbuf[kind, q] + rbuf[kind, (q | bit) - 1]
             bit *= 2
         if q:
-            row_copies[kind, q].start()
-
-    order = (2, 1, 0)
-    for kind in order:
-        for q in range(nr - 1, nr // 2 - 1, -1):
-            reduce(kind, q)
-    for kind in order:
-        for q in range(nr // 2 - 1, -1, -1):
-            reduce(kind, q)
+            for p in range(parts if q == nr // 2 else 1):
+                row_copies[kind, q, p].start()
+
+    def add_last(kind, p):
+        row_copies[kind, nr // 2, p].wait_recv()
+        part = pl.ds(p * size, size)
+        fbuf[kind, 0, part] = fbuf[kind, 0, part] + rbuf[kind, nr // 2 - 1, part]
 
     mirrors = {
-        kind: pltpu.make_async_remote_copy(
-            fbuf.at[kind, 0], mrecv.at[kind - 1], mir_send.at[kind - 1], mir_recv.at[kind - 1],
+        (kind, p): pltpu.make_async_remote_copy(
+            fbuf.at[kind, 0, pl.ds(p * size, size)], mrecv.at[kind - 1, pl.ds(p * size, size)],
+            mir_send.at[kind - 1, p], mir_recv.at[kind - 1, p],
             device_id={"col": near_col if kind == 1 else far_col}, device_id_type=MESH,
         )
         for kind in (1, 2)
+        for p in range(parts)
     }
+
+    def mirror(kind):
+        for p in range(parts):
+            add_last(kind, p)
+            mirrors[kind, p].start()
+
+    sent, kept = range(nr - 1, nr // 2 - 1, -1), range(nr // 2 - 1, -1, -1)
+    order = [(2, q) for q in sent] + [(1, q) for q in sent] + [(2, q) for q in kept]
+    order += [(0, q) for q in sent] + [(1, q) for q in kept] + [(0, q) for q in kept]
+    waiting = []
+    for item in order:
+        group(*item)
+        if item[1] % 2:
+            settle(*item)
+        for held in waiting:
+            settle(*held)
+        waiting = [] if item[1] % 2 else [item]
+        if item == (1, 0):
+            mirror(2)
+    for held in waiting:
+        settle(*held)
+    mirror(1)
     scale = 0.5 / (samples * nr)
     eye = lax.broadcasted_iota(jnp.int32, (BLK, BLK), 0) == lax.broadcasted_iota(jnp.int32, (BLK, BLK), 1)
 
@@ -295,15 +321,14 @@
         out[0, strip[kind], s] = jnp.where(place >= 0, shrunk, 0.0)
 
     def finish_outer(kind):
-        mirrors[kind].wait_recv()
-        for s in range(share):
-            finish(kind, s, mrecv[kind - 1, s].T)
-
-    for kind in (2, 1):
-        add_arrived(kind, 0, nr // 2)
-        mirrors[kind].start()
+        for p in range(parts):
+            mirrors[kind, p].wait_recv()
+            for s in range(p * size, (p + 1) * size):
+                finish(kind, s, mrecv[kind - 1, s].T)
+
     finish_outer(2)
-    add_arrived(0, 0, nr // 2)
+    for p in range(parts):
+        add_last(0, p)
     for s in range(share):
         if paired_here:
             other = s + lax.div(r * share, TB) * (1 - 2 * (s % 2))
@@ -324,6 +349,7 @@
         samples, width = observations.shape
         kmax = omega.shape[2]
         share = kmax // nr
+        parts = 2 if share % 2 == 0 else 1
         vmem, here = pl.BlockSpec(memory_space=pltpu.VMEM), pl.BlockSpec(memory_space=pl.ANY)
         dma = pltpu.SemaphoreType.DMA
         return pl.pallas_call(
@@ -350,13 +376,13 @@
                 dma((CHUNKS,)),
                 dma((CHUNKS,)),
                 dma((CHUNKS,)),
-                dma((3, nr - 1)),
-                dma((3, nr - 1)),
-                dma((2,)),
-                dma((2,)),
+                dma((3, nr - 1, parts)),
+                dma((3, nr - 1, parts)),
+                dma((2, parts)),
+                dma((2, parts)),
             ],
             compiler_params=pltpu.CompilerParams(
-                collective_id=0, has_side_effects=True, vmem_limit_bytes=56 * 1024 * 1024
+                collective_id=0, has_side_effects=True, vmem_limit_bytes=54400 * 1024
             ),
         )(jnp.transpose(block_slots, (1, 0, 2)), observations, omega)
 

time: 64.8 us -> 60.9 us (0.940)
  Pallas kernels: 62.6 us -> 59.1 us
    pallas_call x1, Pallas kernels: 62.6 us -> 59.1 us  [on_device(): pl.pallas_call(functools.partial(kernel, nr, nc, kmax), out_shape=jax.Sha...]
    unnamed x1 -> x3, local copies, waits for them, and re-layouts: 2.06 us -> 1.56 us
where the time goes in v6:
time: 60.9 us; the launch traced here: 60.7 us
  Pallas kernels  59.1 us (97%)
  local copies, waits for them, and re-layouts  1.56 us (3%)
    pallas_call x1, Pallas kernels, on_device(): pl.pallas_call(functools.partial(kernel, nr, nc, kmax), out_shape=jax.Sha...  59.1 us
    unnamed x3, local copies, waits for them, and re-layouts  1.56 us

profile of v6, /device:TPU:0, one launch (start us, length us, event | category | flops | bytes accessed | tf_op | source)
XLA Modules:
  0.0 60.7 jit_solution(3504249057760649027)
XLA Ops:
  0.0 0.0 copy-start
  0.0 0.7 %copy-done = s32[1,3,16]{2,0,1:T(1,128)S(1)} copy-done((s32[1,3,16]{2,0,1:T(1,128)S(1)}, s32[1,3,16]{2,0,1:T(1,128)}, u32[]{:S(2)}) %copy-start) | copy-done | bytes 216
  0.7 59.1 %shard_map.37 = f32[1,3,4,128,128]{4,3,2,1,0:T(8,128)S(1)} custom-call(s32[3,1,16]{2,1,0:T(1,128)S(1)} %bitcast.1, f32[256,1024]{1,0:T(8,128)} %obs_in.1, f32[1,3,16,128,128]{4,3,2,1,0:T(8,128)} %omega_in.1), custom_call_target="tpu_custom_call" | custom-call | tf_op jit(solution)/shard_map/pallas_call | solution.py:355
  59.8 0.9 %copy.5 = f32[1,3,4,128,128]{4,3,2,1,0:T(8,128)} copy(f32[1,3,4,128,128]{4,3,2,1,0:T(8,128)S(1)} %shard_map.37) | data formatting | bytes 1572864
Async XLA Ops:
  0.0 0.7 %copy-start = (s32[1,3,16]{2,0,1:T(1,128)S(1)}, s32[1,3,16]{2,0,1:T(1,128)}, u32[]{:S(2)}) copy-start(s32[1,3,16]{2,0,1:T(1,128)} %param.5) | copy-start | bytes 580

commit v7 on v6

--- a/solution.py
+++ b/solution.py
@@ -36,6 +36,7 @@
 def kernel(
     nr, nc, kmax, slots, obs_in, omega_in, out, tab, obs, omega, near, far, xs, xt, wcat, cum, rs, fbuf, rbuf,
     mrecv, load, near_send, near_recv, far_send, far_recv, row_send, row_recv, mir_send, mir_recv,
+    pre, pre_send, pre_recv,
 ):
     samples = obs_in.shape[0]
     load_obs = pltpu.make_async_copy(obs_in, obs, load.at[0])
@@ -230,6 +231,8 @@
     def row_copy(kind, q, p):
         bit = q & -q
         part = pl.ds(p * size, size) if bit == nr // 2 else pl.ds(0, share)
+        if kind == 1 and q == nr // 2 and paired_here:
+            part = pl.ds(odd * size, size)
         return pltpu.make_async_remote_copy(
             fbuf.at[kind, q, part], rbuf.at[kind, q - 1, part], row_send.at[kind, q - 1, p],
             row_recv.at[kind, q - 1, p], device_id={"row": flip(r, bit)}, device_id_type=MESH,
@@ -239,8 +242,22 @@
         (kind, q, p): row_copy(kind, q, p)
         for kind in range(3)
         for q in range(1, nr)
-        for p in range(parts if q == nr // 2 else 1)
+        for p in range(parts if q == nr // 2 and not (kind == 1 and paired_here) else 1)
     }
+
+    pre_copies = [
+        pltpu.make_async_remote_copy(
+            fbuf.at[1, q, pl.ds((1 - odd) * size, size)], pre.at[i], pre_send.at[i], pre_recv.at[i],
+            device_id={"col": near_col}, device_id_type=MESH,
+        )
+        for i, q in enumerate((nr // 2, 0))
+    ] if paired_here else []
+
+    def add_pair(i, q):
+        pre_copies[i].wait_recv()
+        for s in range(size):
+            at = odd * size + s
+            fbuf[1, q, at] = fbuf[1, q, at] + pre[i, s].T
 
     def group(kind, q):
         first = flip(r, q) * share
@@ -261,7 +278,9 @@
             row_copies[kind, q | bit, 0].wait_recv()
             fbuf[kind, q] = fbuf[kind, q] + rbuf[kind, (q | bit) - 1]
             bit *= 2
-        if q:
+        if kind == 1 and paired_here and q in (0, nr // 2):
+            pre_copies[0 if q else 1].start()
+        elif q:
             for p in range(parts if q == nr // 2 else 1):
                 row_copies[kind, q, p].start()
 
@@ -276,14 +295,19 @@
             mir_send.at[kind - 1, p], mir_recv.at[kind - 1, p],
             device_id={"col": near_col if kind == 1 else far_col}, device_id_type=MESH,
         )
-        for kind in (1, 2)
+        for kind in ((2,) if paired_here else (1, 2))
         for p in range(parts)
     }
 
-    def mirror(kind):
-        for p in range(parts):
-            add_last(kind, p)
-            mirrors[kind, p].start()
+    def mirror(kind, p):
+        add_last(kind, p)
+        mirrors[kind, p].start()
+
+    if paired_here:
+        hand_back = pltpu.make_async_remote_copy(
+            fbuf.at[1, 0, pl.ds(odd * size, size)], mrecv.at[0, pl.ds(odd * size, size)],
+            mir_send.at[0, 0], mir_recv.at[0, 0], device_id={"col": near_col}, device_id_type=MESH,
+        )
 
     sent, kept = range(nr - 1, nr // 2 - 1, -1), range(nr // 2 - 1, -1, -1)
     order = [(2, q) for q in sent] + [(1, q) for q in sent] + [(2, q) for q in kept]
@@ -297,17 +321,32 @@
             settle(*held)
         waiting = [] if item[1] % 2 else [item]
         if item == (1, 0):
-            mirror(2)
+            mirror(2, 0)
+        if item == (0, 1) and paired_here:
+            add_pair(0, nr // 2)
+            row_copies[1, nr // 2, 0].start()
+    for p in range(1, parts):
+        mirror(2, p)
     for held in waiting:
         settle(*held)
-    mirror(1)
+    if paired_here:
+        add_pair(1, 0)
+        row_copies[1, nr // 2, 0].wait_recv()
+        mine = pl.ds(odd * size, size)
+        fbuf[1, 0, mine] = fbuf[1, 0, mine] + rbuf[1, nr // 2 - 1, mine]
+        hand_back.start()
+    else:
+        for p in range(parts):
+            mirror(1, p)
     scale = 0.5 / (samples * nr)
     eye = lax.broadcasted_iota(jnp.int32, (BLK, BLK), 0) == lax.broadcasted_iota(jnp.int32, (BLK, BLK), 1)
 
-    def finish(kind, s, mirrored):
+    def finish(kind, s, mirrored, handed=False):
         slot = r * share + s
         place = position(kind, slot)
-        gradient = fbuf[kind, 0, s] * scale if mirrored is None else (fbuf[kind, 0, s] + mirrored) * scale
+        gradient = mirrored * scale if handed else fbuf[kind, 0, s] * scale
+        if mirrored is not None and not handed:
+            gradient = (fbuf[kind, 0, s] + mirrored) * scale
         old = omega[0, strip[kind], slot]
         edge = step_size * penalty
         if kind == 0:
@@ -335,7 +374,17 @@
             finish(0, s, fbuf[0, 0, other].T)
         else:
             finish(0, s, None)
-    finish_outer(1)
+    if paired_here:
+        for s in range(size):
+            finish(1, odd * size + s, None)
+        hand_back.wait_recv()
+        for s in range(size):
+            at = (1 - odd) * size + s
+            finish(1, at, mrecv[0, at].T, handed=True)
+        for copy in (hand_back, *pre_copies):
+            copy.wait_send()
+    else:
+        finish_outer(1)
     for copy in row_copies.values():
         copy.wait_send()
     for copy in mirrors.values():
@@ -380,6 +429,9 @@
                 dma((3, nr - 1, parts)),
                 dma((2, parts)),
                 dma((2, parts)),
+                pltpu.VMEM((2, max(share // 2, 1), BLK, BLK), f32),
+                dma((2,)),
+                dma((2,)),
             ],
             compiler_params=pltpu.CompilerParams(
                 collective_id=0, has_side_effects=True, vmem_limit_bytes=54400 * 1024

time: 60.9 us -> 60.6 us (level)
  no operation moved by 1% of the time
where the time goes in v7:
time: 60.6 us; the launch traced here: 60.5 us
  Pallas kernels  58.9 us (97%)
  local copies, waits for them, and re-layouts  1.56 us (3%)
    pallas_call x1, Pallas kernels, on_device(): pl.pallas_call(functools.partial(kernel, nr, nc, kmax), out_shape=jax.Sha...  58.9 us
    unnamed x3, local copies, waits for them, and re-layouts  1.56 us

profile of v7, /device:TPU:0, one launch (start us, length us, event | category | flops | bytes accessed | tf_op | source)
XLA Modules:
  0.0 60.5 jit_solution(14857087694911901200)
XLA Ops:
  0.0 0.0 copy-start
  0.0 0.7 %copy-done = s32[1,3,16]{2,0,1:T(1,128)S(1)} copy-done((s32[1,3,16]{2,0,1:T(1,128)S(1)}, s32[1,3,16]{2,0,1:T(1,128)}, u32[]{:S(2)}) %copy-start) | copy-done | bytes 216
  0.7 58.9 %shard_map.37 = f32[1,3,4,128,128]{4,3,2,1,0:T(8,128)S(1)} custom-call(s32[3,1,16]{2,1,0:T(1,128)S(1)} %bitcast.1, f32[256,1024]{1,0:T(8,128)} %obs_in.1, f32[1,3,16,128,128]{4,3,2,1,0:T(8,128)} %omega_in.1), custom_call_target="tpu_custom_call" | custom-call | tf_op jit(solution)/shard_map/pallas_call | solution.py:404
  59.6 0.9 %copy.5 = f32[1,3,4,128,128]{4,3,2,1,0:T(8,128)} copy(f32[1,3,4,128,128]{4,3,2,1,0:T(8,128)S(1)} %shard_map.37) | data formatting | bytes 1572864
Async XLA Ops:
  0.0 0.7 %copy-start = (s32[1,3,16]{2,0,1:T(1,128)S(1)}, s32[1,3,16]{2,0,1:T(1,128)}, u32[]{:S(2)}) copy-start(s32[1,3,16]{2,0,1:T(1,128)} %param.5) | copy-start | bytes 580

commit v8 on v7

--- a/solution.py
+++ b/solution.py
@@ -12,7 +12,7 @@
 TB = 8
 CHUNKS = 16
 STEP = 4
-WINDOW = 4
+WINDOW = 16
 
 step_size = 0.5
 penalty = 0.1

time: 60.6 us -> 60.5 us (level)
  no operation moved by 1% of the time
where the time goes in v8:
time: 60.5 us; the launch traced here: 60.3 us
  Pallas kernels  58.7 us (97%)
  local copies, waits for them, and re-layouts  1.56 us (3%)
    pallas_call x1, Pallas kernels, on_device(): pl.pallas_call(functools.partial(kernel, nr, nc, kmax), out_shape=jax.Sha...  58.7 us
    unnamed x3, local copies, waits for them, and re-layouts  1.56 us

profile of v8, /device:TPU:0, one launch (start us, length us, event | category | flops | bytes accessed | tf_op | source)
XLA Modules:
  0.0 60.3 jit_solution(1104907668380030470)
XLA Ops:
  0.0 0.0 copy-start
  0.0 0.7 %copy-done = s32[1,3,16]{2,0,1:T(1,128)S(1)} copy-done((s32[1,3,16]{2,0,1:T(1,128)S(1)}, s32[1,3,16]{2,0,1:T(1,128)}, u32[]{:S(2)}) %copy-start) | copy-done | bytes 216
  0.7 58.7 %shard_map.37 = f32[1,3,4,128,128]{4,3,2,1,0:T(8,128)S(1)} custom-call(s32[3,1,16]{2,1,0:T(1,128)S(1)} %bitcast.1, f32[256,1024]{1,0:T(8,128)} %obs_in.1, f32[1,3,16,128,128]{4,3,2,1,0:T(8,128)} %omega_in.1), custom_call_target="tpu_custom_call" | custom-call | tf_op jit(solution)/shard_map/pallas_call | solution.py:404
  59.4 0.9 %copy.5 = f32[1,3,4,128,128]{4,3,2,1,0:T(8,128)} copy(f32[1,3,4,128,128]{4,3,2,1,0:T(8,128)S(1)} %shard_map.37) | data formatting | bytes 1572864
Async XLA Ops:
  0.0 0.7 %copy-start = (s32[1,3,16]{2,0,1:T(1,128)S(1)}, s32[1,3,16]{2,0,1:T(1,128)}, u32[]{:S(2)}) copy-start(s32[1,3,16]{2,0,1:T(1,128)} %param.5) | copy-start | bytes 580

commit v9 on v8

--- a/solution.py
+++ b/solution.py
@@ -311,20 +311,29 @@
 
     sent, kept = range(nr - 1, nr // 2 - 1, -1), range(nr // 2 - 1, -1, -1)
     order = [(2, q) for q in sent] + [(1, q) for q in sent] + [(2, q) for q in kept]
-    order += [(0, q) for q in sent] + [(1, q) for q in kept] + [(0, q) for q in kept]
+    if paired_here:
+        order += [(0, q) for q in sent[:-1]] + [(1, q) for q in kept[:-1]]
+        order += [(0, nr // 2), (1, 0)] + [(0, q) for q in kept]
+    else:
+        order += [(0, q) for q in sent] + [(1, q) for q in kept] + [(0, q) for q in kept]
     waiting = []
     for item in order:
+        if paired_here and item == (0, nr // 2):
+            for held in waiting:
+                settle(*held)
+            waiting = []
+            mirror(2, 0)
+            add_pair(0, nr // 2)
+            row_copies[1, nr // 2, 0].start()
         group(*item)
-        if item[1] % 2:
+        at_once = item[1] % 2 or (paired_here and item == (0, nr // 2))
+        if at_once:
             settle(*item)
         for held in waiting:
             settle(*held)
-        waiting = [] if item[1] % 2 else [item]
-        if item == (1, 0):
+        waiting = [] if at_once else [item]
+        if item == (1, 0) and not paired_here:
             mirror(2, 0)
-        if item == (0, 1) and paired_here:
-            add_pair(0, nr // 2)
-            row_copies[1, nr // 2, 0].start()
     for p in range(1, parts):
         mirror(2, p)
     for held in waiting:

time: 60.5 us -> 60.8 us (level)
  no operation moved by 1% of the time
where the time goes in v9:
time: 60.8 us; the launch traced here: 60.6 us
  Pallas kernels  59 us (97%)
  local copies, waits for them, and re-layouts  1.56 us (3%)
    pallas_call x1, Pallas kernels, on_device(): pl.pallas_call(functools.partial(kernel, nr, nc, kmax), out_shape=jax.Sha...  59 us
    unnamed x3, local copies, waits for them, and re-layouts  1.56 us

profile of v9, /device:TPU:0, one launch (start us, length us, event | category | flops | bytes accessed | tf_op | source)
XLA Modules:
  0.0 60.6 jit_solution(3394118697965876934)
XLA Ops:
  0.0 0.0 copy-start
  0.0 0.7 %copy-done = s32[1,3,16]{2,0,1:T(1,128)S(1)} copy-done((s32[1,3,16]{2,0,1:T(1,128)S(1)}, s32[1,3,16]{2,0,1:T(1,128)}, u32[]{:S(2)}) %copy-start) | copy-done | bytes 216
  0.7 59.0 %shard_map.37 = f32[1,3,4,128,128]{4,3,2,1,0:T(8,128)S(1)} custom-call(s32[3,1,16]{2,1,0:T(1,128)S(1)} %bitcast.1, f32[256,1024]{1,0:T(8,128)} %obs_in.1, f32[1,3,16,128,128]{4,3,2,1,0:T(8,128)} %omega_in.1), custom_call_target="tpu_custom_call" | custom-call | tf_op jit(solution)/shard_map/pallas_call | solution.py:413
  59.7 0.9 %copy.5 = f32[1,3,4,128,128]{4,3,2,1,0:T(8,128)} copy(f32[1,3,4,128,128]{4,3,2,1,0:T(8,128)S(1)} %shard_map.37) | data formatting | bytes 1572864
Async XLA Ops:
  0.0 0.7 %copy-start = (s32[1,3,16]{2,0,1:T(1,128)S(1)}, s32[1,3,16]{2,0,1:T(1,128)}, u32[]{:S(2)}) copy-start(s32[1,3,16]{2,0,1:T(1,128)} %param.5) | copy-start | bytes 580

commit v10 on v6

--- a/solution.py
+++ b/solution.py
@@ -10,9 +10,9 @@
 MESH = pl.DeviceIdType.MESH
 BLK = 128
 TB = 8
-CHUNKS = 16
+CHUNKS = 32
 STEP = 4
-WINDOW = 4
+WINDOW = 32
 
 step_size = 0.5
 penalty = 0.1
@@ -165,9 +165,10 @@
 
     def relay_next():
         nonlocal done
-        if done < CHUNKS:
-            relay(done)
-            done += 1
+        for _ in range(2):
+            if done < CHUNKS:
+                relay(done)
+                done += 1
 
     lax.fori_loop(0, 3, fill, 0)
     load_obs.wait()

time: 60.9 us -> 61.1 us (level)
  no operation moved by 1% of the time
where the time goes in v10:
time: 61.1 us; the launch traced here: 60.9 us
  Pallas kernels  59.3 us (97%)
  local copies, waits for them, and re-layouts  1.56 us (3%)
    pallas_call x1, Pallas kernels, on_device(): pl.pallas_call(functools.partial(kernel, nr, nc, kmax), out_shape=jax.Sha...  59.3 us
    unnamed x3, local copies, waits for them, and re-layouts  1.56 us

profile of v10, /device:TPU:0, one launch (start us, length us, event | category | flops | bytes accessed | tf_op | source)
XLA Modules:
  0.0 60.9 jit_solution(11170139517754957462)
XLA Ops:
  0.0 0.0 copy-start
  0.0 0.7 %copy-done = s32[1,3,16]{2,0,1:T(1,128)S(1)} copy-done((s32[1,3,16]{2,0,1:T(1,128)S(1)}, s32[1,3,16]{2,0,1:T(1,128)}, u32[]{:S(2)}) %copy-start) | copy-done | bytes 216
  0.7 59.3 %shard_map.37 = f32[1,3,4,128,128]{4,3,2,1,0:T(8,128)S(1)} custom-call(s32[3,1,16]{2,1,0:T(1,128)S(1)} %bitcast.1, f32[256,1024]{1,0:T(8,128)} %obs_in.1, f32[1,3,16,128,128]{4,3,2,1,0:T(8,128)} %omega_in.1), custom_call_target="tpu_custom_call" | custom-call | tf_op jit(solution)/shard_map/pallas_call | solution.py:356
  60.0 0.9 %copy.5 = f32[1,3,4,128,128]{4,3,2,1,0:T(8,128)} copy(f32[1,3,4,128,128]{4,3,2,1,0:T(8,128)S(1)} %shard_map.37) | data formatting | bytes 1572864
Async XLA Ops:
  0.0 0.7 %copy-start = (s32[1,3,16]{2,0,1:T(1,128)S(1)}, s32[1,3,16]{2,0,1:T(1,128)}, u32[]{:S(2)}) copy-start(s32[1,3,16]{2,0,1:T(1,128)} %param.5) | copy-start | bytes 580

commit v11 on v8

--- a/solution.py
+++ b/solution.py
@@ -186,7 +186,7 @@
     weights(1)
     relay_next()
     weights(2)
-    for first, count in ((0, half), (half, half // 2), (half + half // 2, half // 2)):
+    for first, count in ((0, half), (half, half)):
         relay_to_row(first + count)
         convert(near, 1, first, count)
         relay_next()

time: 60.5 us -> 60.2 us (level)
  no operation moved by 1% of the time
where the time goes in v11:
time: 60.2 us; the launch traced here: 60.1 us
  Pallas kernels  58.5 us (97%)
  local copies, waits for them, and re-layouts  1.56 us (3%)
    pallas_call x1, Pallas kernels, on_device(): pl.pallas_call(functools.partial(kernel, nr, nc, kmax), out_shape=jax.Sha...  58.5 us
    unnamed x3, local copies, waits for them, and re-layouts  1.56 us

profile of v11, /device:TPU:0, one launch (start us, length us, event | category | flops | bytes accessed | tf_op | source)
XLA Modules:
  0.0 60.1 jit_solution(17784421815790174412)
XLA Ops:
  0.0 0.0 copy-start
  0.0 0.7 %copy-done = s32[1,3,16]{2,0,1:T(1,128)S(1)} copy-done((s32[1,3,16]{2,0,1:T(1,128)S(1)}, s32[1,3,16]{2,0,1:T(1,128)}, u32[]{:S(2)}) %copy-start) | copy-done | bytes 216
  0.7 58.5 %shard_map.37 = f32[1,3,4,128,128]{4,3,2,1,0:T(8,128)S(1)} custom-call(s32[3,1,16]{2,1,0:T(1,128)S(1)} %bitcast.1, f32[256,1024]{1,0:T(8,128)} %obs_in.1, f32[1,3,16,128,128]{4,3,2,1,0:T(8,128)} %omega_in.1), custom_call_target="tpu_custom_call" | custom-call | tf_op jit(solution)/shard_map/pallas_call | solution.py:404
  59.2 0.9 %copy.5 = f32[1,3,4,128,128]{4,3,2,1,0:T(8,128)} copy(f32[1,3,4,128,128]{4,3,2,1,0:T(8,128)S(1)} %shard_map.37) | data formatting | bytes 1572864
Async XLA Ops:
  0.0 0.7 %copy-start = (s32[1,3,16]{2,0,1:T(1,128)S(1)}, s32[1,3,16]{2,0,1:T(1,128)}, u32[]{:S(2)}) copy-start(s32[1,3,16]{2,0,1:T(1,128)} %param.5) | copy-start | bytes 580
